TPU v7x, 256 devices: a whole 4x4x8 slice. The times are simulated.
256 devices in a mesh: row: 16 (over z_hi, x), col: 16 (over z_lo, y, core).
Axes of the slice: x: 4, y: 4, z: 8 (z_hi: 4, z_lo: 2; z = z_hi * 2 + z_lo), core: 2. Of those that a mesh axis runs over, the one named last changes fastest.
Arguments:
- alignment: bfloat16 [512, 384, 256], P('row', 'col'), may hold values from -8 to 8
- alignment_mask: int32 [512, 384], P('row', 'col'), may hold values from 0 to 1, as said below
- residue_mask: int32 [384], replicated, may hold values from 0 to 1, as said below
- pair_features: bfloat16 [384, 384, 128], P('row', 'col'), may hold values from -6 to 6
- outer_product_left: bfloat16 [256, 32], replicated, may hold values from -0.375 to 0.375
- outer_product_right: bfloat16 [256, 32], replicated, may hold values from -0.375 to 0.375
- outer_proj: bfloat16 [1024, 128], replicated, may hold values from -0.1875 to 0.1875
- triangle_proj: bfloat16 [128, 512], replicated, may hold values from -0.5 to 0.5
- triangle_gate: bfloat16 [128, 128], replicated, may hold values from -0.5 to 0.5
- triangle_out: bfloat16 [128, 128], replicated, may hold values from -0.5 to 0.5
- transition_in: bfloat16 [128, 512], replicated, may hold values from -0.5 to 0.5
- transition_out: bfloat16 [512, 128], replicated, may hold values from -0.25 to 0.25
Outputs:
- pair_out: bfloat16 [384, 384, 128], P('row', 'col')
Inputs may be any that keep to these rules, and one draw needn't show every extreme that they name: `residue_mask`: masked residues scattered anywhere; at least one residue is masked and at least one takes part. `alignment_mask`: 0 wherever residue_mask is 0.
All inputs are finite; a program needn't handle non-finite values.
Results may differ from a plain program's by a relative error of at most 0.014.
Values may be sent and summed in bfloat16 or wider, within the bound.
A program may use at most 64 MiB of HBM per device.

v0:
```python
import jax
import jax.numpy as jnp
from jax import lax
from jax.sharding import PartitionSpec as P

epsilon = 1e-05


def in_one_piece(arrays, axis, dim, along):
    columns = [a.reshape(*a.shape[:along], -1) for a in arrays]
    both = jnp.concatenate(columns, axis=along)
    filled, at, gathered = (lax.all_gather(both, axis, axis=dim, tiled=True), 0, [])
    for a, column in zip(arrays, columns):
        section = filled[..., at : at + column.shape[along]]
        gathered.append(section.reshape(*section.shape[:along], *a.shape[along:]))
        at += column.shape[along]
    return tuple(gathered)


def in_one_piece_2(arrays, axis, split_dim, concat_dim, along):
    columns = [a.reshape(*a.shape[:along], -1) for a in arrays]
    both = jnp.concatenate(columns, axis=along)
    filled, at, gathered = (
        lax.all_to_all(both, axis, split_axis=split_dim, concat_axis=concat_dim, tiled=True),
        0,
        [],
    )
    for a, column in zip(arrays, columns):
        section = filled[..., at : at + column.shape[along]]
        gathered.append(section.reshape(*section.shape[:along], *a.shape[along:]))
        at += column.shape[along]
    return tuple(gathered)


def sent_to_all(shard, axis):
    copies = jnp.broadcast_to(shard, (lax.axis_size(axis), *shard.shape))
    return lax.all_to_all(copies, axis, split_axis=0, concat_axis=0, tiled=True)


def in_order(blocks, dim):
    blocks = jnp.moveaxis(blocks, 0, dim)
    lengths = blocks.shape
    return blocks.reshape(*lengths[:dim], lengths[dim] * lengths[dim + 1], *lengths[dim + 2 :])


def gather_directly(shard, axis, dim):
    blocks = sent_to_all(shard, axis)
    return in_order(blocks, dim)


def cut_along(shard, dim, devices):
    lengths = shard.shape
    blocks = shard.reshape(*lengths[:dim], devices, lengths[dim] // devices, *lengths[dim + 1 :])
    return jnp.moveaxis(blocks, dim, 0)


def sum_at_owner(shard, axis, dim):
    blocks = cut_along(shard, dim, lax.axis_size(axis))
    arrived = lax.all_to_all(blocks, axis, split_axis=0, concat_axis=0, tiled=True)
    return arrived.astype(jnp.float32).sum(axis=0)


def normalize(values):
    mean_value = jnp.mean(values, axis=-1, keepdims=True)
    centered = values - mean_value
    variance = jnp.mean(centered * centered, axis=-1, keepdims=True)
    return centered * lax.rsqrt(variance + epsilon)


def shards(
    alignment,
    alignment_mask,
    residue_mask,
    pair_features,
    outer_product_left,
    outer_product_right,
    outer_proj,
    triangle_proj,
    triangle_gate,
    triangle_out,
    transition_in,
    transition_out,
):
    block_rows, block_cols, channels = pair_features.shape
    inner = triangle_out.shape[0]
    narrow = outer_product_left.shape[1]
    mask_float = alignment_mask.astype(jnp.float32)
    normed = normalize(alignment.astype(jnp.float32)).astype(jnp.bfloat16)
    left_side = (
        jnp.dot(normed, outer_product_left, preferred_element_type=jnp.float32)
        * mask_float[..., None]
    ).astype(jnp.bfloat16)
    right_side = (
        jnp.dot(normed, outer_product_right, preferred_element_type=jnp.float32)
        * mask_float[..., None]
    ).astype(jnp.bfloat16)
    mask_wire = alignment_mask.astype(jnp.bfloat16)
    right_all, right_mask = in_one_piece((right_side, mask_wire), "row", 0, 2)
    left_rows, left_row_mask = in_one_piece((left_side, mask_wire), "col", 1, 2)
    left_all, left_mask = in_one_piece_2((left_rows, left_row_mask), "row", 1, 0, 2)
    sequences = left_all.shape[0]
    contract = (((0,), (0,)), ((), ()))
    outer = lax.dot_general(
        left_all.reshape(sequences, block_rows * narrow),
        right_all.reshape(sequences, block_cols * narrow),
        contract,
        preferred_element_type=jnp.float32,
    )
    outer = (
        outer.reshape(block_rows, narrow, block_cols, narrow)
        .transpose(0, 2, 1, 3)
        .astype(jnp.bfloat16)
    )
    outer = outer.reshape(block_rows, block_cols, narrow * narrow)
    projected = jnp.dot(outer, outer_proj, preferred_element_type=jnp.float32)
    counts = lax.dot_general(left_mask, right_mask, contract, preferred_element_type=jnp.float32)
    first = (
        pair_features.astype(jnp.float32) + projected / jnp.maximum(counts, 1.0)[..., None]
    ).astype(jnp.bfloat16)
    normed_pair = normalize(first.astype(jnp.float32)).astype(jnp.bfloat16)
    projections = jnp.dot(normed_pair, triangle_proj, preferred_element_type=jnp.float32)
    row_mask = lax.dynamic_slice_in_dim(
        residue_mask, lax.axis_index("row") * block_rows, block_rows
    ).astype(jnp.float32)
    col_mask = lax.dynamic_slice_in_dim(
        residue_mask, lax.axis_index("col") * block_cols, block_cols
    ).astype(jnp.float32)
    pair_mask = (row_mask[:, None] * col_mask[None, :])[..., None]
    left_tri = (
        jax.nn.sigmoid(projections[..., :inner]) * projections[..., inner : 2 * inner] * pair_mask
    ).astype(jnp.bfloat16)
    right_tri = (
        jax.nn.sigmoid(projections[..., 2 * inner : 3 * inner])
        * projections[..., 3 * inner :]
        * pair_mask
    ).astype(jnp.bfloat16)
    right_cols = gather_directly(right_tri, "row", 0)
    summed = sum_at_owner(
        jnp.einsum("ikc,jkc->jic", left_tri, right_cols, preferred_element_type=jnp.float32).astype(
            jnp.bfloat16
        ),
        "col",
        0,
    ).transpose(1, 0, 2)
    normed_sum = normalize(summed).astype(jnp.bfloat16)
    update = jax.nn.sigmoid(
        jnp.dot(normed_pair, triangle_gate, preferred_element_type=jnp.float32)
    ) * jnp.dot(normed_sum, triangle_out, preferred_element_type=jnp.float32)
    second = (first.astype(jnp.float32) + update).astype(jnp.bfloat16)
    normed_second = normalize(second.astype(jnp.float32)).astype(jnp.bfloat16)
    hidden_units = jnp.maximum(
        jnp.dot(normed_second, transition_in, preferred_element_type=jnp.float32), 0.0
    ).astype(jnp.bfloat16)
    return (
        second.astype(jnp.float32)
        + jnp.dot(hidden_units, transition_out, preferred_element_type=jnp.float32)
    ).astype(jnp.bfloat16)


def solution(mesh):
    placed = (
        P("row", "col", None),
        P("row", "col"),
        P(),
        P("row", "col", None),
        P(),
        P(),
        P(),
        P(),
        P(),
        P(),
        P(),
        P(),
    )
    return jax.shard_map(
        shards, mesh=mesh, in_specs=placed, out_specs=P("row", "col", None), check_vma=False
    )
```

profile of v0, /device:TPU:1, one launch (start us, length us, event | category | flops | bytes accessed | tf_op | source)
XLA Modules:
  0.0 312.6 jit_solution(8036478007029515638)
XLA Ops:
  0.0 0.0 copy-start
  0.0 1.2 convert_reduce_fusion.1
  1.2 1.3 fusion.17
  2.6 0.8 convert_bitcast_fusion.2
  3.4 0.1 copy.67
  3.4 0.3 copy.68
  3.7 1.4 fusion.2
  5.1 1.4 fusion.3
  6.6 0.8 pad_maximum_fusion
  7.4 32.7 %all_gather.6 = bf16[32,384,33]{2,1,0:T(8,128)(2,1)S(1)} all-gather(bf16[32,24,33]{2,1,0:T(8,128)(2,1)S(1)} %get-tuple-element.7), channel_id=1, replica_groups=mesh['row'=16,'col'=16] {'col'}, dimensions={1}, use_global_device_ids=true | all-gather | bytes 861696 | tf_op jit(solution)/shard_map/all_gather | solution.py:12
  40.1 2.0 copy.95
  42.1 6.7 %reshape.123 = bf16[16,2,12672]{2,1,0:T(2,128)(2,1)} reshape(bf16[384,32,33]{2,1,0:T(8,128)(2,1)S(1)} %bitcast.88) | data formatting | bytes 1622016
  48.8 8.9 %all-to-all-start = ((bf16[16,2,12672]{2,1,0:T(2,128)(2,1)}), bf16[16,2,12672]{2,1,0:T(2,128)(2,1)}, u32[]{:S(2)}, u32[]{:S(2)}) async-start(bf16[16,2,12672]{2,1,0:T(2,128)(2,1)} %reshape.123), calls=%async_computation | async-start | bytes 1622016 | tf_op jit(solution)/shard_map/all_to_all | solution.py:24
  57.7 89.3 %all_gather.7 = bf16[512,24,33]{2,1,0:T(8,128)(2,1)S(1)} all-gather(bf16[32,24,33]{2,1,0:T(8,128)(2,1)} %get-tuple-element.8), channel_id=1, replica_groups=mesh['row'=16,'col'=16] {'row'}, dimensions={0}, use_global_device_ids=true | all-gather | bytes 861696 | tf_op jit(solution)/shard_map/all_gather | solution.py:12
  147.0 2.6 slice.38
  149.6 4.0 %copy.85 = bf16[512,24,1]{0,1,2:T(8,128)(2,1)S(1)} copy(bf16[512,24,1]{2,1,0:T(8,128)(2,1)} %slice.38) | data formatting | bytes 49152
  153.5 0.0 copy-start.10
  153.5 3.1 %copy.84 = bf16[512,24,32]{0,2,1:T(8,128)(2,1)} copy(bf16[512,24,32]{2,1,0:T(8,128)(2,1)S(1)} %bitcast.86) | data formatting | bytes 1572864
  156.7 0.0 copy-done.10
  156.7 0.1 dynamic-slice_convert_fusion.1
  156.8 0.7 broadcast_multiply_fusion.1
  157.4 0.0 all-to-all-done
  157.4 10.0 %reshape.124 = bf16[384,32,33]{2,1,0:T(8,128)(2,1)} reshape(bf16[16,2,12672]{2,1,0:T(2,128)(2,1)} %all-to-all-done) | data formatting | bytes 1622016
  167.4 5.8 %copy.70 = bf16[32,16,24,33]{0,1,2,3:T(8,128)(2,1)S(1)} copy(bf16[32,16,24,33]{3,0,2,1:T(8,128)(2,1)} %bitcast.89) | data formatting | bytes 1622016 | tf_op jit(solution)/shard_map/all_to_all | solution.py:24
  173.3 3.8 %all_to_all.22 = bf16[512,24,33]{0,1,2:T(8,128)(2,1)} reshape(bf16[16,32,24,33]{1,0,2,3:T(8,128)(2,1)S(1)} %bitcast.87) | data formatting | bytes 1622016 | tf_op jit(solution)/shard_map/all_to_all | solution.py:24
  177.1 1.2 slice.35
  178.3 0.9 convolution_maximum_fusion.1
  179.2 5.4 %convert_bitcast_fusion = bf16[24,24,32,32]{3,2,1,0:T(8,128)(2,1)} fusion(bf16[512,24,32]{0,2,1:T(8,128)(2,1)} %copy.84, bf16[512,24,32]{0,1,2:T(8,128)(2,1)S(1)} %slice.35), kind=kOutput, calls=%fused_computation.1 | convolution fusion | flops 604569600 | bytes 2752512 | tf_op jit(solution)/shard_map/dot_general | solution.py:103
  184.6 6.8 %reshape.108 = bf16[24,24,1024]{2,1,0:T(8,128)(2,1)S(1)} reshape(bf16[24,24,32,32]{3,2,1,0:T(8,128)(2,1)} %convert_bitcast_fusion) | data formatting | bytes 2359296 | tf_op jit(solution)/shard_map/reshape | solution.py:114
  191.4 0.0 copy-done
  191.4 0.0 copy-done.11
  191.4 0.0 copy-start.3
  191.5 0.0 copy-start.8
  191.5 0.6 fusion.52
  192.0 0.0 copy-start.4
  192.0 0.3 multiply_reduce_fusion.2
  192.3 0.4 copy-done.1
  192.7 0.0 copy-done.4
  192.7 0.6 copy-done.6
  193.3 0.0 copy-done.3
  193.3 0.4 fusion.44
  193.7 0.2 fusion.24
  193.9 1.9 broadcast_in_dim.2
  195.8 5.9 %all-to-all-start.1 = ((bf16[16,24,24,128]{3,2,1,0:T(8,128)(2,1)}), bf16[16,24,24,128]{3,2,1,0:T(8,128)(2,1)S(1)}, u32[]{:S(2)}, u32[]{:S(2)}) async-start(bf16[16,24,24,128]{3,2,1,0:T(8,128)(2,1)} %broadcast_in_dim.2), calls=%async_computation.1 | async-start | bytes 4718592 | tf_op jit(solution)/shard_map/all_to_all | solution.py:37
  201.7 0.4 copy.76
  202.1 41.7 %all-to-all-done.1 = bf16[16,24,24,128]{3,2,1,0:T(8,128)(2,1)S(1)} async-done(((bf16[16,24,24,128]{3,2,1,0:T(8,128)(2,1)}), bf16[16,24,24,128]{3,2,1,0:T(8,128)(2,1)S(1)}, u32[]{:S(2)}, u32[]{:S(2)}) %all-to-all-start.1) | async-done | bytes 2359328 | tf_op jit(solution)/shard_map/all_to_all | solution.py:37
  243.8 3.4 %copy.75 = bf16[384,24,128]{0,1,2:T(8,128)(2,1)} copy(bf16[384,24,128]{2,1,0:T(8,128)(2,1)S(1)} %bitcast.90) | data formatting | bytes 4718592 | tf_op jit(solution)/shard_map/reshape | solution.py:43
  247.2 2.6 convert_bitcast_fusion.1
  249.8 3.2 %copy.77 = bf16[384,24,128]{2,1,0:T(8,128)(2,1)} copy(bf16[384,24,128]{0,1,2:T(8,128)(2,1)S(1)} %convert_bitcast_fusion.1) | data formatting | bytes 4718592 | tf_op jit(solution)/shard_map/convert_element_type | solution.py:139
  253.1 24.6 %all-to-all-start.2 = ((bf16[16,24,24,128]{3,2,1,0:T(8,128)(2,1)}), bf16[16,24,24,128]{3,2,1,0:T(8,128)(2,1)S(1)}, u32[]{:S(2)}, u32[]{:S(2)}) async-start(bf16[16,24,24,128]{3,2,1,0:T(8,128)(2,1)} %bitcast.91), calls=%async_computation.2 | async-start | bytes 4718592 | tf_op jit(solution)/shard_map/all_to_all | solution.py:59
  277.7 0.0 copy-start.9
  277.7 0.4 fusion.9
  278.1 30.4 %all-to-all-done.2 = bf16[16,24,24,128]{3,2,1,0:T(8,128)(2,1)S(1)} async-done(((bf16[16,24,24,128]{3,2,1,0:T(8,128)(2,1)}), bf16[16,24,24,128]{3,2,1,0:T(8,128)(2,1)S(1)}, u32[]{:S(2)}, u32[]{:S(2)}) %all-to-all-start.2) | async-done | bytes 2359328 | tf_op jit(solution)/shard_map/all_to_all | solution.py:59
  308.5 0.3 convert_reduce_fusion
  308.8 0.1 bitcast_reduce_fusion
  309.0 0.1 copy.78
  309.0 0.1 copy.79
  309.1 0.3 multiply_reduce_fusion.1
  309.4 0.1 copy.80
  309.5 0.1 copy.81
  309.5 0.2 multiply_convert_fusion.1
  309.8 0.3 fusion.53
  310.1 0.3 multiply_reduce_fusion
  310.4 2.2 fusion.14
  (21 shorter events, 0.1 us)
Async XLA Ops:
  0.0 191.4 %copy-start = (bf16[1024,128]{1,0:T(8,128)(2,1)S(1)}, bf16[1024,128]{1,0:T(8,128)(2,1)}, u32[]{:S(2)}) copy-start(bf16[1024,128]{1,0:T(8,128)(2,1)} %param.18) | copy-start | bytes 786436
  48.8 108.6 %all-to-all-start = ((bf16[16,2,12672]{2,1,0:T(2,128)(2,1)}), bf16[16,2,12672]{2,1,0:T(2,128)(2,1)}, u32[]{:S(2)}, u32[]{:S(2)}) async-start(bf16[16,2,12672]{2,1,0:T(2,128)(2,1)} %reshape.123), calls=%async_computation | async-start | bytes 1622016 | tf_op jit(solution)/shard_map/all_to_all | solution.py:24
  153.5 3.2 %copy-start.10 = (s32[384]{0:T(512)S(1)}, s32[384]{0:T(512)}, u32[]{:S(2)}) copy-start(s32[384]{0:T(512)} %param.14) | copy-start | bytes 4612
  184.6 6.8 %copy-start.11 = (bf16[24,24,128]{2,1,0:T(8,128)(2,1)S(1)}, bf16[24,24,128]{2,1,0:T(8,128)(2,1)}, u32[]{:S(2)}) copy-start(bf16[24,24,128]{2,1,0:T(8,128)(2,1)} %param.15) | copy-start | bytes 442372
  191.4 1.9 copy-start.3
  191.5 2.3 copy-start.8
  192.0 0.7 copy-start.1
  192.0 0.7 copy-start.4
  192.7 0.6 copy-start.6
  195.8 48.0 %all-to-all-start.1 = ((bf16[16,24,24,128]{3,2,1,0:T(8,128)(2,1)}), bf16[16,24,24,128]{3,2,1,0:T(8,128)(2,1)S(1)}, u32[]{:S(2)}, u32[]{:S(2)}) async-start(bf16[16,24,24,128]{3,2,1,0:T(8,128)(2,1)} %broadcast_in_dim.2), calls=%async_computation.1 | async-start | bytes 4718592 | tf_op jit(solution)/shard_map/all_to_all | solution.py:37
  253.0 24.6 %copy-start.2 = (f32[24,24,128]{2,1,0:T(8,128)S(1)}, f32[24,24,128]{2,1,0:T(8,128)}, u32[]{:S(2)}) copy-start(f32[24,24,128]{2,1,0:T(8,128)} %copy-done.1) | copy-start | bytes 884740
  253.0 24.6 %copy-start.5 = (f32[24,24]{1,0:T(8,128)S(1)}, f32[24,24]{1,0:T(8,128)}, u32[]{:S(2)}) copy-start(f32[24,24]{1,0:T(8,128)} %copy-done.4) | copy-start | bytes 6916
  253.1 24.6 %copy-start.7 = (f32[24,24]{1,0:T(8,128)S(1)}, f32[24,24]{1,0:T(8,128)}, u32[]{:S(2)}) copy-start(f32[24,24]{1,0:T(8,128)} %copy-done.6) | copy-start | bytes 6916
  253.1 24.7 %copy-start.12 = (bf16[128,128]{1,0:T(8,128)(2,1)S(1)}, bf16[128,128]{1,0:T(8,128)(2,1)}, u32[]{:S(2)}) copy-start(bf16[128,128]{1,0:T(8,128)(2,1)} %param.20) | copy-start | bytes 98308
  253.1 55.4 %all-to-all-start.2 = ((bf16[16,24,24,128]{3,2,1,0:T(8,128)(2,1)}), bf16[16,24,24,128]{3,2,1,0:T(8,128)(2,1)S(1)}, u32[]{:S(2)}, u32[]{:S(2)}) async-start(bf16[16,24,24,128]{3,2,1,0:T(8,128)(2,1)} %bitcast.91), calls=%async_computation.2 | async-start | bytes 4718592 | tf_op jit(solution)/shard_map/all_to_all | solution.py:59
  277.7 32.1 %copy-start.9 = (bf16[128,128]{1,0:T(8,128)(2,1)S(1)}, bf16[128,128]{1,0:T(8,128)(2,1)}, u32[]{:S(2)}) copy-start(bf16[128,128]{1,0:T(8,128)(2,1)} %param.21) | copy-start | bytes 98308
where the time goes:
time: 314 us; the launch traced here: 313 us
  blocking collectives  122 us (39%)
  waiting for transfers between devices  72.1 us (23%)
  local copies, waits for them, and re-layouts  56.7 us (18%)
  starting transfers between devices  39.4 us (13%)
  matrix products  15.6 us (5%)
  other arithmetic  6.64 us (2%)
    all_gather x2, blocking collectives, in_one_piece(): lax.all_gather(both, axis, axis=dim, tiled=True)  122 us
    all_to_all x1, waiting for transfers between devices, sent_to_all(): return lax.all_to_all(copies, axis, split_axis=0, concat_axis=0, tiled=True)  41.7 us
    all_to_all x1, waiting for transfers between devices, sum_at_owner(): lax.all_to_all(blocks, axis, split_axis=0, concat_axis=0, tiled=True)  30.4 us
    unnamed x30, local copies, waits for them, and re-layouts  24.9 us
    all_to_all x1, starting transfers between devices, sum_at_owner(): lax.all_to_all(blocks, axis, split_axis=0, concat_axis=0, tiled=True)  24.6 us
    all_to_all x2, local copies, waits for them, and re-layouts, in_one_piece_2(): lax.all_to_all(both, axis, split_axis=split_dim, concat_axis=concat_dim,...  9.68 us
    all_to_all x1, starting transfers between devices, in_one_piece_2(): lax.all_to_all(both, axis, split_axis=split_dim, concat_axis=concat_dim,...  8.88 us
    reshape x1, local copies, waits for them, and re-layouts, shards(): outer = outer.reshape(block_rows, block_cols, narrow * narrow)  6.82 us
  transfers between devices with their start and end apart: 3, of which 2 were waited for; matrix products, arithmetic and copies ran while one was open for 4% of the time, Pallas kernels for 0%

commit v1 on v0

v1 whole, which is shorter than its diff:
```python
import jax
import jax.numpy as jnp
from jax import lax
from jax.experimental import pallas as pl
from jax.experimental.pallas import tpu as pltpu
from jax.sharding import PartitionSpec as P

EPSILON = 1e-05
MESH = pl.DeviceIdType.MESH
F32 = jnp.float32
BF16 = jnp.bfloat16
I32 = jnp.int32

LEFT_SCATTER = 0
LEFT_GATHER = 16
RIGHT_GATHER = 33
TRI_SCATTER = 53
TRI_LEFT = 57
TRI_RIGHT = 74
TRANSFERS = 94


def norm(v):
    mean = jnp.mean(v, axis=-1, keepdims=True)
    centered = v - mean
    variance = jnp.mean(centered * centered, axis=-1, keepdims=True)
    return centered * lax.rsqrt(variance + EPSILON)


def dot(a, b):
    return jnp.dot(a, b, preferred_element_type=F32)


def kernel(
    align_ref, amask_ref, rmask_ref, pair_ref, wl_ref, wr_ref, oproj_ref, tproj_ref, tgate_ref,
    tout_ref, tin_ref, trans_ref, out_ref,
    xs, wbd, perm, bd, lnat, left_send, left_all, right_all, left_t, lhs2, pairf, first, normed,
    pmask, proj, gate, tri_left, tri_send, tri_right, rf, summed, ss, rs,
):
    r, q = lax.axis_index("row"), lax.axis_index("col")
    z, x = r // 4, lax.rem(r, 4)
    zl, y, core = q // 8, lax.rem(q // 2, 4), lax.rem(q, 2)
    same = r == q

    def row_of(zz, xx):
        return lax.rem(zz + 4, 4) * 4 + lax.rem(xx + 4, 4)

    def col_of(ll, yy, cc):
        return (ll * 4 + lax.rem(yy + 4, 4)) * 2 + cc

    zp, zm = (row_of(z + 1, x), q), (row_of(z - 1, x), q)
    xp, xm = (row_of(z, x + 1), q), (row_of(z, x - 1), q)
    yp, ym = (r, col_of(zl, y + 1, core)), (r, col_of(zl, y - 1, core))
    zlo = (r, col_of(1 - zl, y, core))
    twin = (r, col_of(zl, y, 1 - core))

    barrier = pltpu.get_barrier_semaphore()
    for device in (zp, zm, xp, xm, yp, ym, zlo, twin):
        pl.semaphore_signal(barrier, inc=1, device_id=device, device_id_type=MESH)

    def greet(t, carry):
        @pl.when(jnp.logical_not(same & (t == r)))
        def _():
            pl.semaphore_signal(barrier, inc=1, device_id=(t, r), device_id_type=MESH)

        return carry

    lax.fori_loop(0, 16, greet, 0)

    def greet_tri(t, carry):
        @pl.when(jnp.logical_not(same & (t * 4 + x == q)))
        def _():
            pl.semaphore_signal(barrier, inc=1, device_id=(q, t * 4 + x), device_id_type=MESH)

        return carry

    lax.fori_loop(0, 4, greet_tri, 0)

    def norm_chunk(t, carry):
        rows = pl.ds(pl.multiple_of(t * 96, 96), 96)
        v = norm(align_ref[rows, :].astype(F32))
        xs[0, rows, :] = v[:, :128]
        xs[1, rows, :] = v[:, 128:]
        return carry

    lax.fori_loop(0, 8, norm_chunk, 0)

    lane = lax.broadcasted_iota(I32, (256, 128), 1)
    spread = (
        lax.rem(lax.broadcasted_iota(I32, (32, 128), 1), 32)
        == lax.broadcasted_iota(I32, (32, 128), 0)
    ).astype(F32).astype(BF16)
    for side, w_ref in enumerate((wl_ref, wr_ref)):
        w = dot(w_ref[...], spread)
        for u in range(4):
            own = (lane >= 32 * u) & (lane < 32 * u + 32)
            wbd[256 * u : 256 * u + 256, 128 * side : 128 * side + 128] = jnp.where(
                own, w, 0.0
            ).astype(BF16)

    lam = lax.broadcasted_iota(I32, (1, 768), 1)
    by24 = (lam * 2731) // 65536
    target = (lam - by24 * 24) * 32 + by24

    def perm_chunk(t, carry):
        start = pl.multiple_of(t * 64, 64)
        rows = lax.broadcasted_iota(I32, (64, 768), 0) + start
        perm[pl.ds(start, 64), :] = (rows == target).astype(F32).astype(BF16)
        return carry

    lax.fori_loop(0, 12, perm_chunk, 0)

    amask = amask_ref[...].astype(F32).astype(BF16)
    row24 = lax.broadcasted_iota(I32, (24, 768), 0) * 32
    lane24 = lax.broadcasted_iota(I32, (24, 768), 1)
    expand = ((lane24 >= row24) & (lane24 < row24 + 32)).astype(F32).astype(BF16)
    mask_wide = dot(amask, expand)
    mask_lanes = dot(
        amask,
        (
            lax.broadcasted_iota(I32, (24, 128), 0) == lax.broadcasted_iota(I32, (24, 128), 1)
        ).astype(F32).astype(BF16),
    ).astype(BF16)
    for g in range(6):
        four = jnp.concatenate(
            [
                xs[half, pl.ds(4 * g + u, 32, stride=24), :].astype(BF16)
                for u in range(4)
                for half in range(2)
            ],
            axis=1,
        )
        both = dot(four, wbd[...])
        m = mask_wide[:, 128 * g : 128 * g + 128]
        lnat[:, 128 * g : 128 * g + 128] = (both[:, :128] * m).astype(BF16)
        right = (both[:, 128:] * m).astype(BF16)
        for h in range(2):
            right_all[h, pl.ds(pl.multiple_of(r * 16, 16), 16), 128 * g : 128 * g + 128] = right[
                16 * h : 16 * h + 16
            ]
    left = dot(lnat[...], perm[...]).astype(BF16)
    for h in range(2):
        right_all[h, pl.ds(pl.multiple_of(r * 16, 16), 16), 768:896] = mask_lanes[
            16 * h : 16 * h + 16
        ]
        for g in range(6):
            left_send[8 * h + g] = left[16 * h : 16 * h + 16, 128 * g : 128 * g + 128]
        left_send[8 * h + 6] = mask_lanes[16 * h : 16 * h + 16]
        left_send[8 * h + 7] = jnp.zeros((16, 128), BF16)

    def remote(src, dst, send, recv, device):
        return pltpu.make_async_remote_copy(
            src_ref=src, dst_ref=dst, send_sem=ss.at[send], recv_sem=rs.at[recv],
            device_id=device, device_id_type=MESH,
        )

    def send(ref, k, device):
        remote(ref, ref, k, k, device).start()

    def wait_recv(ref, k):
        remote(ref, ref, k, k, twin).wait_recv()

    def wait_send(ref, k):
        remote(ref, ref, k, k, twin).wait_send()

    class Ring:
        def __init__(self, slot, half, at, plus, minus, k):
            self.slot, self.half, self.at = slot, half, at
            self.plus, self.minus, self.k = plus, minus, k

        def pos(self, d):
            return lax.rem(self.at + d + 4, 4)

        def start(self):
            send(self.slot(self.at), self.k, self.plus)
            send(self.slot(self.at), self.k + 1, self.minus)

        def from_minus(self):
            wait_recv(self.slot(self.pos(-1)), self.k)
            send(self.half(self.pos(-1), 0), self.k + 2, self.plus)

        def from_plus(self):
            wait_recv(self.slot(self.pos(1)), self.k + 1)
            send(self.half(self.pos(1), 1), self.k + 3, self.minus)

        def finish(self):
            wait_recv(self.half(self.pos(2), 0), self.k + 2)
            wait_recv(self.half(self.pos(2), 1), self.k + 3)

        def drain(self):
            wait_send(self.slot(self.at), self.k)
            wait_send(self.slot(self.at), self.k + 1)
            wait_send(self.half(self.pos(-1), 0), self.k + 2)
            wait_send(self.half(self.pos(1), 1), self.k + 3)

    class Columns:
        def __init__(self, ref, half_rows, k):
            self.ref, self.k = ref, k

            def slot(ll):
                return lambda yy: ref.at[col_of(ll, yy, core)]

            def half(ll):
                return lambda yy, h: ref.at[
                    col_of(ll, yy, core), pl.ds(h * half_rows, half_rows)
                ]

            self.rings = [
                Ring(slot(ll), half(ll), y, yp, ym, k + 1 + 4 * e)
                for e, ll in enumerate((zl, 1 - zl))
            ]
            self.passed = []

        def to_twin(self, ll, yy):
            n = len(self.passed)
            at = lax.rem(yy + 4, 4)
            self.passed.append((ll, at))
            send(self.ref.at[col_of(ll, at, core)], self.k + 9 + n, twin)

        def start(self):
            send(self.ref.at[q], self.k, zlo)
            self.rings[0].start()
            self.to_twin(zl, y)

        def other_half(self):
            wait_recv(self.ref.at[col_of(1 - zl, y, core)], self.k)
            self.rings[1].start()
            self.to_twin(1 - zl, y)

        def from_minus(self, e):
            self.rings[e].from_minus()
            self.to_twin((zl, 1 - zl)[e], y - 1)

        def from_plus(self, e):
            self.rings[e].from_plus()
            self.to_twin((zl, 1 - zl)[e], y + 1)

        def finish(self, e):
            self.rings[e].finish()
            self.to_twin((zl, 1 - zl)[e], y + 2)

        def finish_twin(self):
            for n, (ll, at) in enumerate(self.passed):
                wait_recv(self.ref.at[col_of(ll, at, 1 - core)], self.k + 9 + n)

        def drain(self):
            wait_send(self.ref.at[q], self.k)
            for ring in self.rings:
                ring.drain()
            for n, (ll, at) in enumerate(self.passed):
                wait_send(self.ref.at[col_of(ll, at, core)], self.k + 9 + n)

    class Rows:
        def __init__(self, block, half, k):
            self.zring = Ring(
                lambda zz: block(zz, x), lambda zz, h: half(zz, x, h), z, zp, zm, k
            )

            def slot(zz):
                return lambda xx: block(zz, xx)

            def part(zz):
                return lambda xx, h: half(zz, xx, h)

            self.order = [z, lax.rem(z + 3, 4), lax.rem(z + 1, 4), lax.rem(z + 2, 4)]
            self.xrings = [
                Ring(slot(zz), part(zz), x, xp, xm, k + 4 + 4 * e)
                for e, zz in enumerate(self.order)
            ]

        def start(self):
            self.zring.start()
            self.xrings[0].start()

        def z_neighbours(self):
            self.zring.from_minus()
            self.xrings[1].start()
            self.zring.from_plus()
            self.xrings[2].start()

        def z_far(self):
            self.zring.finish()
            self.xrings[3].start()

        def x_neighbours(self, e):
            self.xrings[e].from_minus()
            self.xrings[e].from_plus()

        def x_far(self, e):
            self.xrings[e].finish()

        def drain(self):
            self.zring.drain()
            for ring in self.xrings:
                ring.drain()

    def right_rows(zz, xx):
        return pl.ds(pl.multiple_of((zz * 4 + xx) * 16, 16), 16)

    right_rows_gather = Rows(
        lambda zz, xx: right_all.at[:, right_rows(zz, xx), :],
        lambda zz, xx, h: right_all.at[pl.ds(h, 1), right_rows(zz, xx), :],
        RIGHT_GATHER,
    )
    left_columns = Columns(left_all, 128, LEFT_GATHER)

    pl.semaphore_wait(barrier, 28 - 2 * same.astype(I32))

    right_rows_gather.start()
    own_rows = pl.ds(pl.multiple_of(r * 16, 16), 16)

    def scatter(t, carry):
        is_self = same & (t == q)

        @pl.when(jnp.logical_not(is_self))
        def _():
            remote(
                left_send.at[t], left_all.at[t, own_rows], LEFT_SCATTER + t, LEFT_SCATTER + r, (q, t)
            ).start()

        @pl.when(is_self)
        def _():
            left_all[t, own_rows] = left_send[t]

        return carry

    lax.fori_loop(0, 16, scatter, 0)

    def zero_chunk(t, carry):
        bd[pl.ds(pl.multiple_of(t * 128, 128), 128), :] = jnp.zeros((128, 512), BF16)
        return carry

    lax.fori_loop(0, 32, zero_chunk, 0)

    def fill_chunk(t, carry):
        block = oproj_ref[pl.ds(pl.multiple_of(t * 32, 32), 32), :]
        for u in range(4):
            bd[pl.ds(pl.multiple_of(t * 128 + 32 * u, 32), 32), 128 * u : 128 * u + 128] = block
        return carry

    lax.fori_loop(0, 32, fill_chunk, 0)

    def scatter_arrived(t, carry):
        @pl.when(jnp.logical_not(same & (t == r)))
        def _():
            piece = left_all.at[q, pl.ds(pl.multiple_of(t * 16, 16), 16)]
            remote(piece, piece, LEFT_SCATTER + t, LEFT_SCATTER + t, twin).wait_recv()

        return carry

    lax.fori_loop(0, 16, scatter_arrived, 0)
    left_columns.start()
    right_rows_gather.z_neighbours()
    left_columns.other_half()

    pairf[...] = pair_ref[...].astype(F32)
    mask_i = jnp.zeros((24, 128), F32)
    sub = lax.broadcasted_iota(I32, (24, 128), 0)
    for i in range(24):
        mask_i = jnp.where(sub == i, rmask_ref[r * 24 + i].astype(F32), mask_i)
    for k in range(24):
        pmask[24 * k : 24 * k + 24, :] = mask_i * rmask_ref[q * 24 + k].astype(F32)

    right_rows_gather.x_neighbours(0)
    left_columns.from_minus(0)
    left_columns.from_plus(0)
    right_rows_gather.z_far()
    right_rows_gather.x_neighbours(1)
    right_rows_gather.x_neighbours(2)
    left_columns.from_minus(1)
    left_columns.from_plus(1)
    left_columns.finish(0)
    left_columns.finish(1)
    right_rows_gather.x_neighbours(3)
    left_columns.finish_twin()

    for h in range(2):
        for g in range(6):
            left_t[128 * g : 128 * g + 128, 256 * h : 256 * h + 256] = left_all[8 * h + g].T
    for e in range(4):
        right_rows_gather.x_far(e)

    counts = sum(
        dot(left_all[8 * h + 6].T, right_all[h, :, 768:896]) for h in range(2)
    )
    counts = jnp.maximum(counts[:24], 1.0)
    for g in range(3):
        rhs = right_all[:, :, 256 * g : 256 * g + 256].reshape(512, 256)
        outer = dot(left_t[...], rhs)
        for u in range(2):
            for c in range(32):
                lhs2[24 * (2 * g + u) : 24 * (2 * g + u) + 24, 128 * c : 128 * c + 128] = outer[
                    24 * c : 24 * c + 24, 128 * u : 128 * u + 128
                ]
    proj[...] = jnp.zeros((144, 512), F32)

    def project(t, carry):
        part = pl.ds(pl.multiple_of(t * 512, 512), 512)
        proj[...] += dot(lhs2[:, part].astype(BF16), bd[part, :])
        return carry

    lax.fori_loop(0, 8, project, 0)
    for g in range(6):
        for u in range(0, 4, 2):
            tiles = []
            for v in (u, u + 1):
                j = 4 * g + v
                tile = pairf[pl.ds(j, 24, stride=24), :] + proj[
                    24 * g : 24 * g + 24, 128 * v : 128 * v + 128
                ] / counts[:, j : j + 1]
                tiles.append(tile)
            rounded = jnp.concatenate(tiles, axis=0).astype(BF16).astype(F32)
            rows = slice(24 * (4 * g + u), 24 * (4 * g + u) + 48)
            first[rows, :] = rounded
            normed[rows, :] = norm(rounded).astype(BF16)

    def operands(t, carry):
        rows = pl.ds(pl.multiple_of(t * 96, 96), 96)
        p = dot(normed[rows, :], tproj_ref[...])
        m = pmask[rows, :]
        tri_left[q, rows, :] = (jax.nn.sigmoid(p[:, :128]) * p[:, 128:256] * m).astype(BF16)
        tri_send[rows, :] = (jax.nn.sigmoid(p[:, 256:384]) * p[:, 384:] * m).astype(BF16)
        return carry

    lax.fori_loop(0, 6, operands, 0)

    tri_columns = Columns(tri_left, 288, TRI_LEFT)
    tri_rows = Rows(
        lambda zz, xx: tri_right.at[xx, zz],
        lambda zz, xx, h: tri_right.at[xx, zz, pl.ds(2 * h, 2)],
        TRI_RIGHT,
    )
    holder, place = lax.rem(q, 4), q // 4

    def tri_scatter(t, carry):
        is_self = same & (t == z)
        piece = pl.ds(pl.multiple_of(t * 144, 144), 144)

        @pl.when(jnp.logical_not(is_self))
        def _():
            remote(
                tri_send.at[piece], tri_right.at[holder, t, place], TRI_SCATTER + t,
                TRI_SCATTER + place, (t * 4 + holder, r),
            ).start()

        @pl.when(is_self)
        def _():
            tri_right[holder, t, place] = tri_send[piece, :]

        return carry

    lax.fori_loop(0, 4, tri_scatter, 0)
    tri_columns.start()

    def tri_arrived(t, carry):
        @pl.when(jnp.logical_not(same & (t == place)))
        def _():
            piece = tri_right.at[x, z, t]
            remote(piece, piece, TRI_SCATTER + t, TRI_SCATTER + t, twin).wait_recv()

        return carry

    lax.fori_loop(0, 4, tri_arrived, 0)
    tri_rows.start()
    tri_columns.other_half()

    def gates(t, carry):
        rows = pl.ds(pl.multiple_of(t * 96, 96), 96)
        gate[rows, :] = jax.nn.sigmoid(dot(normed[rows, :], tgate_ref[...]))
        summed[rows, :] = jnp.zeros((96, 128), F32)
        return carry

    lax.fori_loop(0, 6, gates, 0)

    def accumulate(xx, zz):
        def widen(t, carry):
            rf[pl.ds(pl.multiple_of(t * 144, 144), 144), :] = tri_right[xx, zz, t].astype(F32)
            return carry

        lax.fori_loop(0, 4, widen, 0)
        for half in range(2):
            base = half * 12

            def step(t, acc):
                b, kk = t // 3, lax.rem(t, 3)
                rows = pl.ds(pl.multiple_of(zz * 144 + kk * 48, 16), 48)
                two = tri_left[b * 4 + xx, rows, :].astype(F32)
                acc = list(acc)
                for v in range(2):
                    left = two[24 * v : 24 * v + 24]
                    for j in range(12):
                        row = rf[pl.ds(t * 48 + v * 24 + base + j, 1), :]
                        acc[j] = acc[j] + left * row
                return tuple(acc)

            acc = tuple(summed[24 * (base + j) : 24 * (base + j) + 24, :] for j in range(12))
            acc = lax.fori_loop(0, 12, step, acc)
            for j in range(12):
                summed[24 * (base + j) : 24 * (base + j) + 24, :] = acc[j]

    def xat(d):
        return lax.rem(x + d + 4, 4)

    tri_rows.z_neighbours()
    tri_columns.from_minus(0)
    tri_columns.from_plus(0)
    tri_rows.x_neighbours(0)
    tri_rows.z_far()
    tri_columns.from_minus(1)
    tri_columns.from_plus(1)
    tri_columns.finish(0)
    tri_columns.finish(1)
    tri_rows.x_neighbours(1)
    tri_columns.finish_twin()
    order = tri_rows.order
    accumulate(x, order[0])
    accumulate(x, order[1])
    tri_rows.x_neighbours(2)
    accumulate(x, order[2])
    accumulate(x, order[3])
    accumulate(xat(-1), order[0])
    accumulate(xat(1), order[0])
    tri_rows.x_neighbours(3)
    accumulate(xat(-1), order[1])
    accumulate(xat(1), order[1])
    accumulate(xat(-1), order[2])
    accumulate(xat(1), order[2])
    accumulate(xat(-1), order[3])
    accumulate(xat(1), order[3])
    for e in range(4):
        tri_rows.x_far(e)
        accumulate(xat(2), order[e])

    def finish(t, carry):
        rows = pl.ds(pl.multiple_of(t * 96, 96), 96)
        normed_sum = norm(summed[rows, :]).astype(BF16)
        second = (first[rows, :] + gate[rows, :] * dot(normed_sum, tout_ref[...])).astype(BF16)
        second = second.astype(F32)
        hidden = jnp.maximum(dot(norm(second).astype(BF16), tin_ref[...]), 0.0).astype(BF16)
        pairf[rows, :] = second + dot(hidden, trans_ref[...])
        return carry

    lax.fori_loop(0, 6, finish, 0)
    for i in range(0, 24, 2):
        out_ref[24 * i : 24 * i + 48, :] = jnp.concatenate(
            [pairf[pl.ds(i + v, 24, stride=24), :] for v in range(2)], axis=0
        ).astype(BF16)

    def scatter_left(t, carry):
        @pl.when(jnp.logical_not(same & (t == q)))
        def _():
            remote(
                left_send.at[t], left_send.at[t], LEFT_SCATTER + t, LEFT_SCATTER + t, twin
            ).wait_send()

        return carry

    lax.fori_loop(0, 16, scatter_left, 0)

    def tri_left_here(t, carry):
        @pl.when(jnp.logical_not(same & (t == z)))
        def _():
            piece = tri_send.at[pl.ds(pl.multiple_of(t * 144, 144), 144)]
            remote(piece, piece, TRI_SCATTER + t, TRI_SCATTER + t, twin).wait_send()

        return carry

    lax.fori_loop(0, 4, tri_left_here, 0)
    left_columns.drain()
    right_rows_gather.drain()
    tri_columns.drain()
    tri_rows.drain()


def shards(alignment, alignment_mask, residue_mask, pair_features, *weights):
    vmem = pl.BlockSpec(memory_space=pltpu.VMEM)
    smem = pl.BlockSpec(memory_space=pltpu.SMEM)
    out = pl.pallas_call(
        kernel,
        out_shape=jax.ShapeDtypeStruct((576, 128), BF16),
        in_specs=[vmem, vmem, smem] + [vmem] * 9,
        out_specs=vmem,
        scratch_shapes=[
            pltpu.VMEM((2, 768, 128), F32),
            pltpu.VMEM((1024, 256), BF16),
            pltpu.VMEM((768, 768), BF16),
            pltpu.VMEM((4096, 512), BF16),
            pltpu.VMEM((32, 768), BF16),
            pltpu.VMEM((16, 16, 128), BF16),
            pltpu.VMEM((16, 256, 128), BF16),
            pltpu.VMEM((2, 256, 896), BF16),
            pltpu.VMEM((768, 512), BF16),
            pltpu.VMEM((144, 4096), F32),
            pltpu.VMEM((576, 128), F32),
            pltpu.VMEM((576, 128), F32),
            pltpu.VMEM((576, 128), BF16),
            pltpu.VMEM((576, 128), F32),
            pltpu.VMEM((144, 512), F32),
            pltpu.VMEM((576, 128), F32),
            pltpu.VMEM((16, 576, 128), BF16),
            pltpu.VMEM((576, 128), BF16),
            pltpu.VMEM((4, 4, 4, 144, 128), BF16),
            pltpu.VMEM((576, 128), F32),
            pltpu.VMEM((576, 128), F32),
            pltpu.SemaphoreType.DMA((TRANSFERS,)),
            pltpu.SemaphoreType.DMA((TRANSFERS,)),
        ],
        compiler_params=pltpu.CompilerParams(
            collective_id=0, has_side_effects=True, vmem_limit_bytes=48 * 1024 * 1024
        ),
        cost_estimate=pl.CostEstimate(
            flops=1_500_000_000, bytes_accessed=2_000_000, transcendentals=400_000
        ),
    )(
        alignment.reshape(768, 256), alignment_mask, residue_mask, pair_features.reshape(576, 128),
        *weights,
    )
    return out.reshape(24, 24, 128)


def solution(mesh):
    placed = (P("row", "col", None), P("row", "col"), P(), P("row", "col", None)) + (P(),) * 8
    return jax.shard_map(
        shards, mesh=mesh, in_specs=placed, out_specs=P("row", "col", None), check_vma=False
    )
```

time: 314 us -> 100 us (0.32)
  blocking collectives: 122 us -> 0 us
  Pallas kernels: 0 us -> 91.1 us
  waiting for transfers between devices: 72.1 us -> 0 us
  local copies, waits for them, and re-layouts: 56.7 us -> 8.59 us
  starting transfers between devices: 39.4 us -> 0 us
  matrix products: 15.6 us -> 0 us
  other arithmetic: 6.64 us -> 0 us
    all_gather x2 -> x0, blocking collectives: 122 us -> none  [in_one_piece(): lax.all_gather(both, axis, axis=dim, tiled=True)]
    pallas_call x0 -> x1, Pallas kernels: none -> 91.1 us  [shards(): pl.pallas_call(kernel, out_shape=jax.ShapeDtypeStruct((576, 128), BF16),...]
    all_to_all x3 -> x0, waiting for transfers between devices: 72.1 us -> none  [the longest x1 41.7 us: sent_to_all(): return lax.all_to_all(copies, axis, split_axis=0, concat_axis=0, tiled=True)]
    all_to_all x3 -> x0, starting transfers between devices: 39.4 us -> none  [the longest x1 24.6 us: sum_at_owner(): lax.all_to_all(blocks, axis, split_axis=0, concat_axis=0, tiled=True)]
    unnamed x30 -> x22, local copies, waits for them, and re-layouts: 24.9 us -> 8.59 us
    dot_general x10 -> x0, matrix products: 15.6 us -> none  [the longest x1 5.42 us: shards(): lax.dot_general(left_all.reshape(sequences, block_rows * narrow), right_a...]
    reshape x3 -> x0, local copies, waits for them, and re-layouts: 10.4 us -> none  [the longest x1 6.82 us: shards(): outer = outer.reshape(block_rows, block_cols, narrow * narrow)]
    all_to_all x2 -> x0, local copies, waits for them, and re-layouts: 9.68 us -> none  [in_one_piece_2(): lax.all_to_all(both, axis, split_axis=split_dim, concat_axis=concat_dim,...]
  transfers between devices with their start and end apart: 3 -> 0, of which waited for: 2 -> 0; matrix products, arithmetic and copies ran while one was open for 4% -> 0% of each run, Pallas kernels for 0% -> 0%
where the time goes in v1:
time: 100 us; the launch traced here: 99.8 us
  Pallas kernels  91.1 us (91%)
  local copies, waits for them, and re-layouts  8.59 us (9%)
    pallas_call x1, Pallas kernels, shards(): pl.pallas_call(kernel, out_shape=jax.ShapeDtypeStruct((576, 128), BF16),...  91.1 us
    unnamed x22, local copies, waits for them, and re-layouts  8.59 us

profile of v1, /device:TPU:1, one launch (start us, length us, event | category | flops | bytes accessed | tf_op | source)
XLA Modules:
  0.0 99.8 jit_solution(15144919143984803661)
XLA Ops:
  0.0 0.0 copy-start.2
  0.0 0.8 copy.13.amask_ref
  0.8 0.8 copy.14.wl_ref
  1.7 0.0 copy-start.6
  1.7 0.0 copy-start.8
  1.7 0.8 copy.15.wr_ref
  2.5 0.0 copy-done.2
  2.5 0.0 copy-done.6
  2.5 0.0 copy-done.8
  2.6 0.0 copy-start
  2.6 1.0 copy-done
  3.6 0.0 copy-start.1
  3.6 0.9 copy-done.1
  4.5 0.0 copy-start.3
  4.5 0.9 copy-done.3
  5.4 0.0 copy-start.4
  5.4 0.9 copy-done.4
  6.3 0.0 copy-start.5
  6.3 0.9 copy-done.5
  7.2 0.0 copy-start.7
  7.2 0.8 copy-done.7
  8.0 91.1 %shard_map.118 = bf16[576,128]{1,0:T(8,128)(2,1)S(1)} custom-call(bf16[768,256]{1,0:T(8,128)(2,1)S(1)} %bitcast.4, s32[32,24]{1,0:T(8,128)S(1)} %copy.13.amask_ref, s32[384]{0:T(512)S(1)} %copy-done.8, bf16[576,128]{1,0:T(8,128)(2,1)S(1)} %bitcast.5, bf16[256,32]{1,0:T(8,128)(2,1)S(1)} %copy.14.wl_ref, bf16[256,32]{1,0:T(8,128)(2,1)S(1)} %copy.15.wr_ref, ...), custom_call_target="tpu_custom_call" | custom-call | flops 1500000000 | bytes 2000000 | tf_op jit(solution)/shard_map/pallas_call | solution.py:578
  99.1 0.7 copy.17
Async XLA Ops:
  0.0 2.5 %copy-start.2 = (bf16[24,24,128]{2,1,0:T(8,128)(2,1)S(1)}, bf16[24,24,128]{2,1,0:T(8,128)(2,1)}, u32[]{:S(2)}) copy-start(bf16[24,24,128]{2,1,0:T(8,128)(2,1)} %param.15) | copy-start | bytes 442372
  1.7 0.9 copy-start.6
  1.7 0.9 copy-start.8
  2.6 1.0 %copy-start = (bf16[32,24,256]{2,1,0:T(8,128)(2,1)S(1)}, bf16[32,24,256]{2,1,0:T(8,128)(2,1)}, u32[]{:S(2)}) copy-start(bf16[32,24,256]{2,1,0:T(8,128)(2,1)} %param.12) | copy-start | bytes 1179652
  3.6 0.9 copy-start.1
  4.5 0.9 copy-start.3
  5.4 0.9 copy-start.4
  6.3 0.9 copy-start.5
  7.2 0.8 copy-start.7

commit v2 on v1

--- a/solution.py
+++ b/solution.py
@@ -32,11 +32,32 @@
 
 
 def kernel(
+    align_hbm, amask_hbm, rmask_hbm, pair_hbm, wl_hbm, wr_hbm, oproj_hbm, tproj_hbm, tgate_hbm,
+    tout_hbm, tin_hbm, trans_hbm, out_ref,
     align_ref, amask_ref, rmask_ref, pair_ref, wl_ref, wr_ref, oproj_ref, tproj_ref, tgate_ref,
-    tout_ref, tin_ref, trans_ref, out_ref,
-    xs, wbd, perm, bd, lnat, left_send, left_all, right_all, left_t, lhs2, pairf, first, normed,
-    pmask, proj, gate, tri_left, tri_send, tri_right, rf, summed, ss, rs,
+    tout_ref, tin_ref, trans_ref,
+    xs, wbd, perm, bd, lnat, left_send, left_all, right_all, left_t, lhs2, ptile, first, normed,
+    pmask, gate, tri_left, tri_send, tri_right, lf, rf, part, ss, rs, ls,
 ):
+    loads = {
+        name: pltpu.make_async_copy(src, dst, ls.at[n])
+        for n, (name, src, dst) in enumerate(
+            (
+                ("align", align_hbm, align_ref),
+                ("wl", wl_hbm, wl_ref),
+                ("wr", wr_hbm, wr_ref),
+                ("amask", amask_hbm, amask_ref),
+                ("oproj", oproj_hbm, oproj_ref),
+                ("rmask", rmask_hbm, rmask_ref),
+                ("pair", pair_hbm, pair_ref),
+                ("tproj", tproj_hbm, tproj_ref),
+                ("tgate", tgate_hbm, tgate_ref),
+                ("tout", tout_hbm, tout_ref),
+                ("tin", tin_hbm, tin_ref),
+                ("trans", trans_hbm, trans_ref),
+            )
+        )
+    }
     r, q = lax.axis_index("row"), lax.axis_index("col")
     z, x = r // 4, lax.rem(r, 4)
     zl, y, core = q // 8, lax.rem(q // 2, 4), lax.rem(q, 2)
@@ -76,6 +97,11 @@
 
     lax.fori_loop(0, 4, greet_tri, 0)
 
+    for load in loads.values():
+        load.start()
+
+    loads["align"].wait()
+
     def norm_chunk(t, carry):
         rows = pl.ds(pl.multiple_of(t * 96, 96), 96)
         v = norm(align_ref[rows, :].astype(F32))
@@ -90,8 +116,10 @@
         lax.rem(lax.broadcasted_iota(I32, (32, 128), 1), 32)
         == lax.broadcasted_iota(I32, (32, 128), 0)
     ).astype(F32).astype(BF16)
+    loads["wl"].wait()
+    loads["wr"].wait()
     for side, w_ref in enumerate((wl_ref, wr_ref)):
-        w = dot(w_ref[...], spread)
+        w = dot(w_ref[...].astype(F32).T.astype(BF16), spread)
         for u in range(4):
             own = (lane >= 32 * u) & (lane < 32 * u + 32)
             wbd[256 * u : 256 * u + 256, 128 * side : 128 * side + 128] = jnp.where(
@@ -110,7 +138,8 @@
 
     lax.fori_loop(0, 12, perm_chunk, 0)
 
-    amask = amask_ref[...].astype(F32).astype(BF16)
+    loads["amask"].wait()
+    amask = amask_ref[...].astype(F32).T.astype(BF16)
     row24 = lax.broadcasted_iota(I32, (24, 768), 0) * 32
     lane24 = lax.broadcasted_iota(I32, (24, 768), 1)
     expand = ((lane24 >= row24) & (lane24 < row24 + 32)).astype(F32).astype(BF16)
@@ -304,33 +333,13 @@
     )
     left_columns = Columns(left_all, 128, LEFT_GATHER)
 
-    pl.semaphore_wait(barrier, 28 - 2 * same.astype(I32))
-
-    right_rows_gather.start()
-    own_rows = pl.ds(pl.multiple_of(r * 16, 16), 16)
-
-    def scatter(t, carry):
-        is_self = same & (t == q)
-
-        @pl.when(jnp.logical_not(is_self))
-        def _():
-            remote(
-                left_send.at[t], left_all.at[t, own_rows], LEFT_SCATTER + t, LEFT_SCATTER + r, (q, t)
-            ).start()
-
-        @pl.when(is_self)
-        def _():
-            left_all[t, own_rows] = left_send[t]
-
-        return carry
-
-    lax.fori_loop(0, 16, scatter, 0)
-
     def zero_chunk(t, carry):
         bd[pl.ds(pl.multiple_of(t * 128, 128), 128), :] = jnp.zeros((128, 512), BF16)
+        part[pl.ds(pl.multiple_of(t * 144, 144), 144), :] = jnp.zeros((144, 128), F32)
         return carry
 
     lax.fori_loop(0, 32, zero_chunk, 0)
+    loads["oproj"].wait()
 
     def fill_chunk(t, carry):
         block = oproj_ref[pl.ds(pl.multiple_of(t * 32, 32), 32), :]
@@ -339,6 +348,37 @@
         return carry
 
     lax.fori_loop(0, 32, fill_chunk, 0)
+    loads["rmask"].wait()
+    mask_k = jnp.zeros((24, 128), F32)
+    sub = lax.broadcasted_iota(I32, (24, 128), 0)
+    for k in range(24):
+        mask_k = jnp.where(sub == k, rmask_ref[q * 24 + k].astype(F32), mask_k)
+    for i in range(24):
+        pmask[24 * i : 24 * i + 24, :] = mask_k * rmask_ref[r * 24 + i].astype(F32)
+    for name in ("pair", "tproj", "tgate", "tout", "tin", "trans"):
+        loads[name].wait()
+
+    pl.semaphore_wait(barrier, 28 - 2 * same.astype(I32))
+
+    right_rows_gather.start()
+    own_rows = pl.ds(pl.multiple_of(r * 16, 16), 16)
+
+    def scatter(t, carry):
+        is_self = same & (t == q)
+
+        @pl.when(jnp.logical_not(is_self))
+        def _():
+            remote(
+                left_send.at[t], left_all.at[t, own_rows], LEFT_SCATTER + t, LEFT_SCATTER + r, (q, t)
+            ).start()
+
+        @pl.when(is_self)
+        def _():
+            left_all[t, own_rows] = left_send[t]
+
+        return carry
+
+    lax.fori_loop(0, 16, scatter, 0)
 
     def scatter_arrived(t, carry):
         @pl.when(jnp.logical_not(same & (t == r)))
@@ -352,14 +392,6 @@
     left_columns.start()
     right_rows_gather.z_neighbours()
     left_columns.other_half()
-
-    pairf[...] = pair_ref[...].astype(F32)
-    mask_i = jnp.zeros((24, 128), F32)
-    sub = lax.broadcasted_iota(I32, (24, 128), 0)
-    for i in range(24):
-        mask_i = jnp.where(sub == i, rmask_ref[r * 24 + i].astype(F32), mask_i)
-    for k in range(24):
-        pmask[24 * k : 24 * k + 24, :] = mask_i * rmask_ref[q * 24 + k].astype(F32)
 
     right_rows_gather.x_neighbours(0)
     left_columns.from_minus(0)
@@ -389,40 +421,31 @@
         outer = dot(left_t[...], rhs)
         for u in range(2):
             for c in range(32):
-                lhs2[24 * (2 * g + u) : 24 * (2 * g + u) + 24, 128 * c : 128 * c + 128] = outer[
+                lhs2[32 * (2 * g + u) : 32 * (2 * g + u) + 24, 128 * c : 128 * c + 128] = outer[
                     24 * c : 24 * c + 24, 128 * u : 128 * u + 128
-                ]
-    proj[...] = jnp.zeros((144, 512), F32)
-
-    def project(t, carry):
-        part = pl.ds(pl.multiple_of(t * 512, 512), 512)
-        proj[...] += dot(lhs2[:, part].astype(BF16), bd[part, :])
-        return carry
-
-    lax.fori_loop(0, 8, project, 0)
-    for g in range(6):
-        for u in range(0, 4, 2):
-            tiles = []
-            for v in (u, u + 1):
-                j = 4 * g + v
-                tile = pairf[pl.ds(j, 24, stride=24), :] + proj[
-                    24 * g : 24 * g + 24, 128 * v : 128 * v + 128
-                ] / counts[:, j : j + 1]
-                tiles.append(tile)
-            rounded = jnp.concatenate(tiles, axis=0).astype(BF16).astype(F32)
-            rows = slice(24 * (4 * g + u), 24 * (4 * g + u) + 48)
-            first[rows, :] = rounded
-            normed[rows, :] = norm(rounded).astype(BF16)
-
-    def operands(t, carry):
-        rows = pl.ds(pl.multiple_of(t * 96, 96), 96)
+                ].astype(BF16)
+    for n in range(2):
+        proj = dot(lhs2[...], bd[:, 256 * n : 256 * n + 256])
+        for g in range(6):
+            for u in range(2):
+                j = 4 * g + 2 * n + u
+                ptile[24 * j : 24 * j + 24, :] = (
+                    proj[32 * g : 32 * g + 24, 128 * u : 128 * u + 128] / counts[:, j : j + 1]
+                )
+    for i in range(0, 24, 2):
+        rows = slice(24 * i, 24 * i + 48)
+        tiles = [ptile[pl.ds(i + v, 24, stride=24), :] for v in range(2)]
+        rounded = (pair_ref[rows, :].astype(F32) + jnp.concatenate(tiles, axis=0)).astype(BF16)
+        rounded = rounded.astype(F32)
+        first[rows, :] = rounded
+        normed[rows, :] = norm(rounded).astype(BF16)
+
+    for t in range(3):
+        rows = slice(192 * t, 192 * t + 192)
         p = dot(normed[rows, :], tproj_ref[...])
         m = pmask[rows, :]
         tri_left[q, rows, :] = (jax.nn.sigmoid(p[:, :128]) * p[:, 128:256] * m).astype(BF16)
         tri_send[rows, :] = (jax.nn.sigmoid(p[:, 256:384]) * p[:, 384:] * m).astype(BF16)
-        return carry
-
-    lax.fori_loop(0, 6, operands, 0)
 
     tri_columns = Columns(tri_left, 288, TRI_LEFT)
     tri_rows = Rows(
@@ -464,39 +487,44 @@
     tri_rows.start()
     tri_columns.other_half()
 
-    def gates(t, carry):
-        rows = pl.ds(pl.multiple_of(t * 96, 96), 96)
-        gate[rows, :] = jax.nn.sigmoid(dot(normed[rows, :], tgate_ref[...]))
-        summed[rows, :] = jnp.zeros((96, 128), F32)
-        return carry
-
-    lax.fori_loop(0, 6, gates, 0)
+    gate[...] = jax.nn.sigmoid(dot(normed[...], tgate_ref[...]))
+
+    def widen_left(xx):
+        def widen(t, carry):
+            b, rows = t // 4, pl.ds(pl.multiple_of(lax.rem(t, 4) * 144, 144), 144)
+            lf[xx, b, rows, :] = tri_left[b * 4 + xx, rows, :].astype(F32)
+            return carry
+
+        lax.fori_loop(0, 16, widen, 0)
 
     def accumulate(xx, zz):
         def widen(t, carry):
-            rf[pl.ds(pl.multiple_of(t * 144, 144), 144), :] = tri_right[xx, zz, t].astype(F32)
+            rf[t] = tri_right[xx, zz, t].astype(F32)
             return carry
 
         lax.fori_loop(0, 4, widen, 0)
-        for half in range(2):
-            base = half * 12
-
-            def step(t, acc):
-                b, kk = t // 3, lax.rem(t, 3)
-                rows = pl.ds(pl.multiple_of(zz * 144 + kk * 48, 16), 48)
-                two = tri_left[b * 4 + xx, rows, :].astype(F32)
-                acc = list(acc)
-                for v in range(2):
-                    left = two[24 * v : 24 * v + 24]
-                    for j in range(12):
-                        row = rf[pl.ds(t * 48 + v * 24 + base + j, 1), :]
-                        acc[j] = acc[j] + left * row
-                return tuple(acc)
-
-            acc = tuple(summed[24 * (base + j) : 24 * (base + j) + 24, :] for j in range(12))
-            acc = lax.fori_loop(0, 12, step, acc)
-            for j in range(12):
-                summed[24 * (base + j) : 24 * (base + j) + 24, :] = acc[j]
+
+        def block(t, carry):
+            def at(u, v):
+                return pl.ds(pl.multiple_of(((t * 4 + u) * 24 + zz * 6 + v) * 8, 8), 8)
+
+            acc = [[part[at(u, v), :] for v in range(6)] for u in range(4)]
+            for b in range(4):
+                for k in range(3):
+                    left = [
+                        lf[xx, b, pl.ds(pl.multiple_of((t * 4 + u) * 24 + 8 * k, 8), 8), :]
+                        for u in range(4)
+                    ]
+                    right = [rf[b, 24 * v + 8 * k : 24 * v + 8 * k + 8, :] for v in range(6)]
+                    for u in range(4):
+                        for v in range(6):
+                            acc[u][v] = acc[u][v] + left[u] * right[v]
+            for u in range(4):
+                for v in range(6):
+                    part[at(u, v), :] = acc[u][v]
+            return carry
+
+        lax.fori_loop(0, 6, block, 0)
 
     def xat(d):
         return lax.rem(x + d + 4, 4)
@@ -513,11 +541,14 @@
     tri_rows.x_neighbours(1)
     tri_columns.finish_twin()
     order = tri_rows.order
+    widen_left(x)
     accumulate(x, order[0])
     accumulate(x, order[1])
     tri_rows.x_neighbours(2)
     accumulate(x, order[2])
     accumulate(x, order[3])
+    widen_left(xat(-1))
+    widen_left(xat(1))
     accumulate(xat(-1), order[0])
     accumulate(xat(1), order[0])
     tri_rows.x_neighbours(3)
@@ -527,24 +558,21 @@
     accumulate(xat(1), order[2])
     accumulate(xat(-1), order[3])
     accumulate(xat(1), order[3])
+    widen_left(xat(2))
     for e in range(4):
         tri_rows.x_far(e)
         accumulate(xat(2), order[e])
 
-    def finish(t, carry):
-        rows = pl.ds(pl.multiple_of(t * 96, 96), 96)
-        normed_sum = norm(summed[rows, :]).astype(BF16)
+    for t in range(2):
+        rows = slice(288 * t, 288 * t + 288)
+        summed = part[pl.ds(2304 * t, 288, stride=8), :]
+        for k in range(1, 8):
+            summed = summed + part[pl.ds(2304 * t + k, 288, stride=8), :]
+        normed_sum = norm(summed).astype(BF16)
         second = (first[rows, :] + gate[rows, :] * dot(normed_sum, tout_ref[...])).astype(BF16)
         second = second.astype(F32)
         hidden = jnp.maximum(dot(norm(second).astype(BF16), tin_ref[...]), 0.0).astype(BF16)
-        pairf[rows, :] = second + dot(hidden, trans_ref[...])
-        return carry
-
-    lax.fori_loop(0, 6, finish, 0)
-    for i in range(0, 24, 2):
-        out_ref[24 * i : 24 * i + 48, :] = jnp.concatenate(
-            [pairf[pl.ds(i + v, 24, stride=24), :] for v in range(2)], axis=0
-        ).astype(BF16)
+        out_ref[rows, :] = (second + dot(hidden, trans_ref[...])).astype(BF16)
 
     def scatter_left(t, carry):
         @pl.when(jnp.logical_not(same & (t == q)))
@@ -574,13 +602,25 @@
 
 def shards(alignment, alignment_mask, residue_mask, pair_features, *weights):
     vmem = pl.BlockSpec(memory_space=pltpu.VMEM)
-    smem = pl.BlockSpec(memory_space=pltpu.SMEM)
+    hbm = pl.BlockSpec(memory_space=pltpu.HBM)
     out = pl.pallas_call(
         kernel,
         out_shape=jax.ShapeDtypeStruct((576, 128), BF16),
-        in_specs=[vmem, vmem, smem] + [vmem] * 9,
+        in_specs=[hbm] * 12,
         out_specs=vmem,
         scratch_shapes=[
+            pltpu.VMEM((768, 256), BF16),
+            pltpu.VMEM((24, 32), I32),
+            pltpu.SMEM((384,), I32),
+            pltpu.VMEM((576, 128), BF16),
+            pltpu.VMEM((32, 256), BF16),
+            pltpu.VMEM((32, 256), BF16),
+            pltpu.VMEM((1024, 128), BF16),
+            pltpu.VMEM((128, 512), BF16),
+            pltpu.VMEM((128, 128), BF16),
+            pltpu.VMEM((128, 128), BF16),
+            pltpu.VMEM((128, 512), BF16),
+            pltpu.VMEM((512, 128), BF16),
             pltpu.VMEM((2, 768, 128), F32),
             pltpu.VMEM((1024, 256), BF16),
             pltpu.VMEM((768, 768), BF16),
@@ -590,30 +630,31 @@
             pltpu.VMEM((16, 256, 128), BF16),
             pltpu.VMEM((2, 256, 896), BF16),
             pltpu.VMEM((768, 512), BF16),
-            pltpu.VMEM((144, 4096), F32),
+            pltpu.VMEM((192, 4096), BF16),
             pltpu.VMEM((576, 128), F32),
             pltpu.VMEM((576, 128), F32),
             pltpu.VMEM((576, 128), BF16),
             pltpu.VMEM((576, 128), F32),
-            pltpu.VMEM((144, 512), F32),
             pltpu.VMEM((576, 128), F32),
             pltpu.VMEM((16, 576, 128), BF16),
             pltpu.VMEM((576, 128), BF16),
             pltpu.VMEM((4, 4, 4, 144, 128), BF16),
-            pltpu.VMEM((576, 128), F32),
-            pltpu.VMEM((576, 128), F32),
+            pltpu.VMEM((4, 4, 576, 128), F32),
+            pltpu.VMEM((4, 144, 128), F32),
+            pltpu.VMEM((4608, 128), F32),
             pltpu.SemaphoreType.DMA((TRANSFERS,)),
             pltpu.SemaphoreType.DMA((TRANSFERS,)),
+            pltpu.SemaphoreType.DMA((12,)),
         ],
         compiler_params=pltpu.CompilerParams(
-            collective_id=0, has_side_effects=True, vmem_limit_bytes=48 * 1024 * 1024
+            collective_id=0, has_side_effects=True, vmem_limit_bytes=60 * 1024 * 1024
         ),
         cost_estimate=pl.CostEstimate(
             flops=1_500_000_000, bytes_accessed=2_000_000, transcendentals=400_000
         ),
     )(
-        alignment.reshape(768, 256), alignment_mask, residue_mask, pair_features.reshape(576, 128),
-        *weights,
+        alignment.reshape(768, 256), alignment_mask.T, residue_mask, pair_features.reshape(576, 128),
+        weights[0].T, weights[1].T, *weights[2:],
     )
     return out.reshape(24, 24, 128)
 

time: 100 us -> 81.9 us (0.82)
  Pallas kernels: 91.1 us -> 80.2 us
  local copies, waits for them, and re-layouts: 8.59 us -> 1.59 us
    pallas_call x1, Pallas kernels: 91.1 us -> 80.2 us  [shards(): pl.pallas_call(kernel, out_shape=jax.ShapeDtypeStruct((576, 128), BF16),...]
    unnamed x22 -> x1, local copies, waits for them, and re-layouts: 8.59 us -> 1.59 us
where the time goes in v2:
time: 81.9 us; the launch traced here: 81.8 us
  Pallas kernels  80.2 us (98%)
  local copies, waits for them, and re-layouts  1.59 us (2%)
    pallas_call x1, Pallas kernels, shards(): pl.pallas_call(kernel, out_shape=jax.ShapeDtypeStruct((576, 128), BF16),...  80.2 us

profile of v2, /device:TPU:1, one launch (start us, length us, event | category | flops | bytes accessed | tf_op | source)
XLA Modules:
  0.0 81.8 jit_solution(2577654740239065619)
XLA Ops:
  0.0 80.2 %shard_map.118 = bf16[576,128]{1,0:T(8,128)(2,1)} custom-call(bf16[768,256]{1,0:T(8,128)(2,1)} %bitcast.7, s32[24,32]{1,0:T(8,128)} %bitcast.11, s32[384]{0:T(512)} %rmask_hbm.1, bf16[576,128]{1,0:T(8,128)(2,1)} %bitcast.8, bf16[32,256]{1,0:T(8,128)(2,1)} %bitcast.9, bf16[32,256]{1,0:T(8,128)(2,1)} %bitcast.10, bf16[1024,128]{1,0:T(8,128)(2,1)} %oproj_hbm.1, ...), custom_call_target="tpu_custom_call" | custom-call | flops 1500000000 | bytes 2000000 | tf_op jit(solution)/shard_map/pallas_call | solution.py:606
  80.2 1.6 %copy.14 = bf16[24,24,128]{2,1,0:T(8,128)(2,1)} copy(bf16[24,24,128]{2,1,0:T(8,128)(2,1)} %bitcast.6) | data formatting | bytes 294912

commit v3 on v2

--- a/solution.py
+++ b/solution.py
@@ -12,12 +12,12 @@
 I32 = jnp.int32
 
 LEFT_SCATTER = 0
-LEFT_GATHER = 16
-RIGHT_GATHER = 33
-TRI_SCATTER = 53
-TRI_LEFT = 57
-TRI_RIGHT = 74
-TRANSFERS = 94
+LEFT_GATHER = 4
+RIGHT_GATHER = 21
+TRI_SCATTER = 41
+TRI_LEFT = 45
+TRI_RIGHT = 62
+TRANSFERS = 102
 
 
 def norm(v):
@@ -74,19 +74,22 @@
     yp, ym = (r, col_of(zl, y + 1, core)), (r, col_of(zl, y - 1, core))
     zlo = (r, col_of(1 - zl, y, core))
     twin = (r, col_of(zl, y, 1 - core))
+    dp, dm = (r, col_of(1 - zl, y + 1, core)), (r, col_of(1 - zl, y - 1, core))
 
     barrier = pltpu.get_barrier_semaphore()
-    for device in (zp, zm, xp, xm, yp, ym, zlo, twin):
+    for device in (zp, zm, xp, xm, yp, ym, zlo, twin, dp, dm):
         pl.semaphore_signal(barrier, inc=1, device_id=device, device_id_type=MESH)
 
     def greet(t, carry):
-        @pl.when(jnp.logical_not(same & (t == r)))
-        def _():
-            pl.semaphore_signal(barrier, inc=1, device_id=(t, r), device_id_type=MESH)
-
-        return carry
-
-    lax.fori_loop(0, 16, greet, 0)
+        @pl.when(jnp.logical_not(same & (t == z)))
+        def _():
+            pl.semaphore_signal(
+                barrier, inc=1, device_id=(t * 4 + lax.rem(q, 4), r), device_id_type=MESH
+            )
+
+        return carry
+
+    lax.fori_loop(0, 4, greet, 0)
 
     def greet_tri(t, carry):
         @pl.when(jnp.logical_not(same & (t * 4 + x == q)))
@@ -150,6 +153,7 @@
             lax.broadcasted_iota(I32, (24, 128), 0) == lax.broadcasted_iota(I32, (24, 128), 1)
         ).astype(F32).astype(BF16),
     ).astype(BF16)
+    own_rows = pl.ds(pl.multiple_of((x * 4 + z) * 32, 32), 32)
     for g in range(6):
         four = jnp.concatenate(
             [
@@ -163,19 +167,13 @@
         m = mask_wide[:, 128 * g : 128 * g + 128]
         lnat[:, 128 * g : 128 * g + 128] = (both[:, :128] * m).astype(BF16)
         right = (both[:, 128:] * m).astype(BF16)
-        for h in range(2):
-            right_all[h, pl.ds(pl.multiple_of(r * 16, 16), 16), 128 * g : 128 * g + 128] = right[
-                16 * h : 16 * h + 16
-            ]
+        right_all[own_rows, 128 * g : 128 * g + 128] = right
     left = dot(lnat[...], perm[...]).astype(BF16)
-    for h in range(2):
-        right_all[h, pl.ds(pl.multiple_of(r * 16, 16), 16), 768:896] = mask_lanes[
-            16 * h : 16 * h + 16
-        ]
-        for g in range(6):
-            left_send[8 * h + g] = left[16 * h : 16 * h + 16, 128 * g : 128 * g + 128]
-        left_send[8 * h + 6] = mask_lanes[16 * h : 16 * h + 16]
-        left_send[8 * h + 7] = jnp.zeros((16, 128), BF16)
+    right_all[own_rows, 768:896] = mask_lanes
+    for g in range(6):
+        left_send[g // 2, g % 2] = left[:, 128 * g : 128 * g + 128]
+    left_send[3, 0] = mask_lanes
+    left_send[3, 1] = jnp.zeros((32, 128), BF16)
 
     def remote(src, dst, send, recv, device):
         return pltpu.make_async_remote_copy(
@@ -223,8 +221,8 @@
             wait_send(self.half(self.pos(1), 1), self.k + 3)
 
     class Columns:
-        def __init__(self, ref, half_rows, k):
-            self.ref, self.k = ref, k
+        def __init__(self, ref, half_rows, k, diagonal):
+            self.ref, self.k, self.diagonal = ref, k, diagonal
 
             def slot(ll):
                 return lambda yy: ref.at[col_of(ll, yy, core)]
@@ -249,11 +247,15 @@
         def start(self):
             send(self.ref.at[q], self.k, zlo)
             self.rings[0].start()
+            if self.diagonal:
+                send(self.ref.at[q], self.rings[1].k, dp)
+                send(self.ref.at[q], self.rings[1].k + 1, dm)
             self.to_twin(zl, y)
 
         def other_half(self):
             wait_recv(self.ref.at[col_of(1 - zl, y, core)], self.k)
-            self.rings[1].start()
+            if not self.diagonal:
+                self.rings[1].start()
             self.to_twin(1 - zl, y)
 
         def from_minus(self, e):
@@ -323,15 +325,15 @@
             for ring in self.xrings:
                 ring.drain()
 
-    def right_rows(zz, xx):
-        return pl.ds(pl.multiple_of((zz * 4 + xx) * 16, 16), 16)
+    def right_rows(zz, xx, h, count):
+        return pl.ds(pl.multiple_of((xx * 4 + zz) * 32 + 16 * h, 16), count)
 
     right_rows_gather = Rows(
-        lambda zz, xx: right_all.at[:, right_rows(zz, xx), :],
-        lambda zz, xx, h: right_all.at[pl.ds(h, 1), right_rows(zz, xx), :],
+        lambda zz, xx: right_all.at[right_rows(zz, xx, 0, 32)],
+        lambda zz, xx, h: right_all.at[right_rows(zz, xx, h, 16)],
         RIGHT_GATHER,
     )
-    left_columns = Columns(left_all, 128, LEFT_GATHER)
+    left_columns = Columns(left_all, 2, LEFT_GATHER, True)
 
     def zero_chunk(t, carry):
         bd[pl.ds(pl.multiple_of(t * 128, 128), 128), :] = jnp.zeros((128, 512), BF16)
@@ -358,67 +360,69 @@
     for name in ("pair", "tproj", "tgate", "tout", "tin", "trans"):
         loads[name].wait()
 
-    pl.semaphore_wait(barrier, 28 - 2 * same.astype(I32))
-
+    pl.semaphore_wait(barrier, 18 - 2 * same.astype(I32))
+
+    def scatter(t, carry):
+        is_self = same & (t == z)
+        p = t * 4 + x
+
+        @pl.when(jnp.logical_not(is_self))
+        def _():
+            remote(
+                left_send.at[t], left_all.at[p, z], LEFT_SCATTER + t, LEFT_SCATTER + z, (q, p)
+            ).start()
+
+        @pl.when(is_self)
+        def _():
+            left_all[p, z] = left_send[t]
+
+        return carry
+
+    lax.fori_loop(0, 4, scatter, 0)
     right_rows_gather.start()
-    own_rows = pl.ds(pl.multiple_of(r * 16, 16), 16)
-
-    def scatter(t, carry):
-        is_self = same & (t == q)
-
-        @pl.when(jnp.logical_not(is_self))
-        def _():
-            remote(
-                left_send.at[t], left_all.at[t, own_rows], LEFT_SCATTER + t, LEFT_SCATTER + r, (q, t)
-            ).start()
-
-        @pl.when(is_self)
-        def _():
-            left_all[t, own_rows] = left_send[t]
-
-        return carry
-
-    lax.fori_loop(0, 16, scatter, 0)
 
     def scatter_arrived(t, carry):
-        @pl.when(jnp.logical_not(same & (t == r)))
-        def _():
-            piece = left_all.at[q, pl.ds(pl.multiple_of(t * 16, 16), 16)]
+        @pl.when(jnp.logical_not(same & (t == z)))
+        def _():
+            piece = left_all.at[q, t]
             remote(piece, piece, LEFT_SCATTER + t, LEFT_SCATTER + t, twin).wait_recv()
 
         return carry
 
-    lax.fori_loop(0, 16, scatter_arrived, 0)
+    lax.fori_loop(0, 4, scatter_arrived, 0)
     left_columns.start()
     right_rows_gather.z_neighbours()
+    right_rows_gather.x_neighbours(0)
     left_columns.other_half()
-
-    right_rows_gather.x_neighbours(0)
-    left_columns.from_minus(0)
-    left_columns.from_plus(0)
+    for e in range(2):
+        left_columns.from_minus(e)
+        left_columns.from_plus(e)
     right_rows_gather.z_far()
     right_rows_gather.x_neighbours(1)
     right_rows_gather.x_neighbours(2)
-    left_columns.from_minus(1)
-    left_columns.from_plus(1)
     left_columns.finish(0)
     left_columns.finish(1)
     right_rows_gather.x_neighbours(3)
     left_columns.finish_twin()
 
-    for h in range(2):
-        for g in range(6):
-            left_t[128 * g : 128 * g + 128, 256 * h : 256 * h + 256] = left_all[8 * h + g].T
+    for g in range(6):
+        for m in range(4):
+            left_t[128 * g : 128 * g + 128, 128 * m : 128 * m + 128] = (
+                left_all[4 * (g // 2) + m, :, g % 2].reshape(128, 128).T
+            )
     for e in range(4):
         right_rows_gather.x_far(e)
 
     counts = sum(
-        dot(left_all[8 * h + 6].T, right_all[h, :, 768:896]) for h in range(2)
+        dot(
+            left_all[12 + m, :, 0].reshape(128, 128).T,
+            right_all[128 * m : 128 * m + 128, 768:896],
+        )
+        for m in range(4)
     )
     counts = jnp.maximum(counts[:24], 1.0)
     for g in range(3):
-        rhs = right_all[:, :, 256 * g : 256 * g + 256].reshape(512, 256)
-        outer = dot(left_t[...], rhs)
+        outer = dot(left_t[...], right_all[:, 256 * g : 256 * g + 256])
         for u in range(2):
             for c in range(32):
                 lhs2[32 * (2 * g + u) : 32 * (2 * g + u) + 24, 128 * c : 128 * c + 128] = outer[
@@ -447,12 +451,16 @@
         tri_left[q, rows, :] = (jax.nn.sigmoid(p[:, :128]) * p[:, 128:256] * m).astype(BF16)
         tri_send[rows, :] = (jax.nn.sigmoid(p[:, 256:384]) * p[:, 384:] * m).astype(BF16)
 
-    tri_columns = Columns(tri_left, 288, TRI_LEFT)
-    tri_rows = Rows(
-        lambda zz, xx: tri_right.at[xx, zz],
-        lambda zz, xx, h: tri_right.at[xx, zz, pl.ds(2 * h, 2)],
-        TRI_RIGHT,
-    )
+    tri_columns = Columns(tri_left, 288, TRI_LEFT, False)
+
+    def chunk(n):
+        return Rows(
+            lambda zz, xx: tri_right.at[xx, zz, pl.ds(2 * n, 2)],
+            lambda zz, xx, h: tri_right.at[xx, zz, pl.ds(2 * n + h, 1)],
+            TRI_RIGHT + 20 * n,
+        )
+
+    rows0, rows1 = chunk(0), chunk(1)
     holder, place = lax.rem(q, 4), q // 4
 
     def tri_scatter(t, carry):
@@ -484,7 +492,8 @@
         return carry
 
     lax.fori_loop(0, 4, tri_arrived, 0)
-    tri_rows.start()
+    rows0.start()
+    rows1.start()
     tri_columns.other_half()
 
     gate[...] = jax.nn.sigmoid(dot(normed[...], tgate_ref[...]))
@@ -529,38 +538,40 @@
     def xat(d):
         return lax.rem(x + d + 4, 4)
 
-    tri_rows.z_neighbours()
     tri_columns.from_minus(0)
     tri_columns.from_plus(0)
-    tri_rows.x_neighbours(0)
-    tri_rows.z_far()
+    rows0.z_neighbours()
+    rows0.x_neighbours(0)
+    rows1.z_neighbours()
+    rows1.x_neighbours(0)
     tri_columns.from_minus(1)
     tri_columns.from_plus(1)
+    rows0.z_far()
     tri_columns.finish(0)
+    rows0.x_neighbours(1)
+    rows0.x_neighbours(2)
+    rows1.z_far()
     tri_columns.finish(1)
-    tri_rows.x_neighbours(1)
+    rows1.x_neighbours(1)
     tri_columns.finish_twin()
-    order = tri_rows.order
+    order = rows0.order
     widen_left(x)
     accumulate(x, order[0])
+    rows1.x_neighbours(2)
+    rows0.x_neighbours(3)
     accumulate(x, order[1])
-    tri_rows.x_neighbours(2)
     accumulate(x, order[2])
+    rows1.x_neighbours(3)
     accumulate(x, order[3])
-    widen_left(xat(-1))
-    widen_left(xat(1))
-    accumulate(xat(-1), order[0])
-    accumulate(xat(1), order[0])
-    tri_rows.x_neighbours(3)
-    accumulate(xat(-1), order[1])
-    accumulate(xat(1), order[1])
-    accumulate(xat(-1), order[2])
-    accumulate(xat(1), order[2])
-    accumulate(xat(-1), order[3])
-    accumulate(xat(1), order[3])
+    for d in (-1, 1):
+        widen_left(xat(d))
+    for e in range(4):
+        for d in (-1, 1):
+            accumulate(xat(d), order[e])
     widen_left(xat(2))
     for e in range(4):
-        tri_rows.x_far(e)
+        rows0.x_far(e)
+        rows1.x_far(e)
         accumulate(xat(2), order[e])
 
     for t in range(2):
@@ -575,7 +586,7 @@
         out_ref[rows, :] = (second + dot(hidden, trans_ref[...])).astype(BF16)
 
     def scatter_left(t, carry):
-        @pl.when(jnp.logical_not(same & (t == q)))
+        @pl.when(jnp.logical_not(same & (t == z)))
         def _():
             remote(
                 left_send.at[t], left_send.at[t], LEFT_SCATTER + t, LEFT_SCATTER + t, twin
@@ -583,7 +594,7 @@
 
         return carry
 
-    lax.fori_loop(0, 16, scatter_left, 0)
+    lax.fori_loop(0, 4, scatter_left, 0)
 
     def tri_left_here(t, carry):
         @pl.when(jnp.logical_not(same & (t == z)))
@@ -597,7 +608,8 @@
     left_columns.drain()
     right_rows_gather.drain()
     tri_columns.drain()
-    tri_rows.drain()
+    rows0.drain()
+    rows1.drain()
 
 
 def shards(alignment, alignment_mask, residue_mask, pair_features, *weights):
@@ -626,9 +638,9 @@
             pltpu.VMEM((768, 768), BF16),
             pltpu.VMEM((4096, 512), BF16),
             pltpu.VMEM((32, 768), BF16),
-            pltpu.VMEM((16, 16, 128), BF16),
-            pltpu.VMEM((16, 256, 128), BF16),
-            pltpu.VMEM((2, 256, 896), BF16),
+            pltpu.VMEM((4, 2, 32, 128), BF16),
+            pltpu.VMEM((16, 4, 2, 32, 128), BF16),
+            pltpu.VMEM((512, 896), BF16),
             pltpu.VMEM((768, 512), BF16),
             pltpu.VMEM((192, 4096), BF16),
             pltpu.VMEM((576, 128), F32),

time: 81.9 us -> 79.9 us (0.976)
  the two profiles are of different devices: /device:TPU:1 before, /device:TPU:18 now
where the time goes in v3:
time: 79.9 us; the launch traced here: 79.8 us
  Pallas kernels  78.2 us (98%)
  local copies, waits for them, and re-layouts  1.59 us (2%)
    pallas_call x1, Pallas kernels, shards(): pl.pallas_call(kernel, out_shape=jax.ShapeDtypeStruct((576, 128), BF16),...  78.2 us

profile of v3, /device:TPU:18, one launch (start us, length us, event | category | flops | bytes accessed | tf_op | source)
XLA Modules:
  0.0 79.8 jit_solution(18003532284315294398)
XLA Ops:
  0.0 78.2 %shard_map.118 = bf16[576,128]{1,0:T(8,128)(2,1)} custom-call(bf16[768,256]{1,0:T(8,128)(2,1)} %bitcast.7, s32[24,32]{1,0:T(8,128)} %bitcast.11, s32[384]{0:T(512)} %rmask_hbm.1, bf16[576,128]{1,0:T(8,128)(2,1)} %bitcast.8, bf16[32,256]{1,0:T(8,128)(2,1)} %bitcast.9, bf16[32,256]{1,0:T(8,128)(2,1)} %bitcast.10, bf16[1024,128]{1,0:T(8,128)(2,1)} %oproj_hbm.1, ...), custom_call_target="tpu_custom_call" | custom-call | flops 1500000000 | bytes 2000000 | tf_op jit(solution)/shard_map/pallas_call | solution.py:618
  78.2 1.6 %copy.14 = bf16[24,24,128]{2,1,0:T(8,128)(2,1)} copy(bf16[24,24,128]{2,1,0:T(8,128)(2,1)} %bitcast.6) | data formatting | bytes 294912

commit v4 on v3

--- a/solution.py
+++ b/solution.py
@@ -77,9 +77,6 @@
     dp, dm = (r, col_of(1 - zl, y + 1, core)), (r, col_of(1 - zl, y - 1, core))
 
     barrier = pltpu.get_barrier_semaphore()
-    for device in (zp, zm, xp, xm, yp, ym, zlo, twin, dp, dm):
-        pl.semaphore_signal(barrier, inc=1, device_id=device, device_id_type=MESH)
-
     def greet(t, carry):
         @pl.when(jnp.logical_not(same & (t == z)))
         def _():
@@ -89,7 +86,8 @@
 
         return carry
 
-    lax.fori_loop(0, 4, greet, 0)
+    for t in range(4):
+        greet(t, 0)
 
     def greet_tri(t, carry):
         @pl.when(jnp.logical_not(same & (t * 4 + x == q)))
@@ -98,7 +96,10 @@
 
         return carry
 
-    lax.fori_loop(0, 4, greet_tri, 0)
+    for t in range(4):
+        greet_tri(t, 0)
+    for device in (zp, zm, xp, xm, yp, ym, zlo, twin, dp, dm):
+        pl.semaphore_signal(barrier, inc=1, device_id=device, device_id_type=MESH)
 
     for load in loads.values():
         load.start()
@@ -392,17 +393,18 @@
     lax.fori_loop(0, 4, scatter_arrived, 0)
     left_columns.start()
     right_rows_gather.z_neighbours()
+    left_columns.other_half()
+    left_columns.from_minus(0)
+    left_columns.from_plus(0)
     right_rows_gather.x_neighbours(0)
-    left_columns.other_half()
-    for e in range(2):
-        left_columns.from_minus(e)
-        left_columns.from_plus(e)
     right_rows_gather.z_far()
+    left_columns.from_minus(1)
+    left_columns.from_plus(1)
     right_rows_gather.x_neighbours(1)
     right_rows_gather.x_neighbours(2)
     left_columns.finish(0)
+    right_rows_gather.x_neighbours(3)
     left_columns.finish(1)
-    right_rows_gather.x_neighbours(3)
     left_columns.finish_twin()
 
     for g in range(6):
@@ -446,10 +448,8 @@
 
     for t in range(3):
         rows = slice(192 * t, 192 * t + 192)
-        p = dot(normed[rows, :], tproj_ref[...])
-        m = pmask[rows, :]
-        tri_left[q, rows, :] = (jax.nn.sigmoid(p[:, :128]) * p[:, 128:256] * m).astype(BF16)
-        tri_send[rows, :] = (jax.nn.sigmoid(p[:, 256:384]) * p[:, 384:] * m).astype(BF16)
+        p = dot(normed[rows, :], tproj_ref[:, 256:])
+        tri_send[rows, :] = (jax.nn.sigmoid(p[:, :128]) * p[:, 128:] * pmask[rows, :]).astype(BF16)
 
     tri_columns = Columns(tri_left, 288, TRI_LEFT, False)
 
@@ -481,6 +481,12 @@
         return carry
 
     lax.fori_loop(0, 4, tri_scatter, 0)
+    for t in range(3):
+        rows = slice(192 * t, 192 * t + 192)
+        p = dot(normed[rows, :], tproj_ref[:, :256])
+        tri_left[q, rows, :] = (
+            jax.nn.sigmoid(p[:, :128]) * p[:, 128:] * pmask[rows, :]
+        ).astype(BF16)
     tri_columns.start()
 
     def tri_arrived(t, carry):
@@ -542,43 +548,51 @@
     tri_columns.from_plus(0)
     rows0.z_neighbours()
     rows0.x_neighbours(0)
+    tri_columns.from_minus(1)
+    tri_columns.from_plus(1)
     rows1.z_neighbours()
     rows1.x_neighbours(0)
-    tri_columns.from_minus(1)
-    tri_columns.from_plus(1)
+    tri_columns.finish(0)
     rows0.z_far()
-    tri_columns.finish(0)
+    tri_columns.finish(1)
     rows0.x_neighbours(1)
     rows0.x_neighbours(2)
-    rows1.z_far()
-    tri_columns.finish(1)
-    rows1.x_neighbours(1)
     tri_columns.finish_twin()
     order = rows0.order
     widen_left(x)
     accumulate(x, order[0])
+    rows1.z_far()
+    rows1.x_neighbours(1)
+    accumulate(x, order[1])
     rows1.x_neighbours(2)
-    rows0.x_neighbours(3)
-    accumulate(x, order[1])
     accumulate(x, order[2])
-    rows1.x_neighbours(3)
     accumulate(x, order[3])
     for d in (-1, 1):
         widen_left(xat(d))
-    for e in range(4):
-        for d in (-1, 1):
-            accumulate(xat(d), order[e])
+    accumulate(xat(-1), order[0])
+    rows0.x_neighbours(3)
+    accumulate(xat(1), order[0])
+    accumulate(xat(-1), order[1])
+    rows1.x_neighbours(3)
+    accumulate(xat(1), order[1])
+    accumulate(xat(-1), order[2])
+    accumulate(xat(1), order[2])
     widen_left(xat(2))
-    for e in range(4):
+    for e in range(3):
         rows0.x_far(e)
         rows1.x_far(e)
         accumulate(xat(2), order[e])
-
-    for t in range(2):
-        rows = slice(288 * t, 288 * t + 288)
-        summed = part[pl.ds(2304 * t, 288, stride=8), :]
+    accumulate(xat(-1), order[3])
+    accumulate(xat(1), order[3])
+    rows0.x_far(3)
+    rows1.x_far(3)
+    accumulate(xat(2), order[3])
+
+    for t in range(1):
+        rows = slice(576 * t, 576 * t + 576)
+        summed = part[pl.ds(2304 * t, 576, stride=8), :]
         for k in range(1, 8):
-            summed = summed + part[pl.ds(2304 * t + k, 288, stride=8), :]
+            summed = summed + part[pl.ds(2304 * t + k, 576, stride=8), :]
         normed_sum = norm(summed).astype(BF16)
         second = (first[rows, :] + gate[rows, :] * dot(normed_sum, tout_ref[...])).astype(BF16)
         second = second.astype(F32)

time: 79.9 us -> 76.2 us (0.954)
  the two profiles are of different devices: /device:TPU:18 before, /device:TPU:1 now
where the time goes in v4:
time: 76.2 us; the launch traced here: 75.2 us
  Pallas kernels  73.6 us (97%)
  local copies, waits for them, and re-layouts  1.59 us (2%)
    pallas_call x1, Pallas kernels, shards(): pl.pallas_call(kernel, out_shape=jax.ShapeDtypeStruct((576, 128), BF16),...  73.6 us
    unnamed x1, local copies, waits for them, and re-layouts  1.59 us

profile of v4, /device:TPU:1, one launch (start us, length us, event | category | flops | bytes accessed | tf_op | source)
XLA Modules:
  0.0 75.2 jit_solution(10476213464743757052)
XLA Ops:
  0.0 73.6 %shard_map.118 = bf16[576,128]{1,0:T(8,128)(2,1)} custom-call(bf16[768,256]{1,0:T(8,128)(2,1)} %bitcast.7, s32[24,32]{1,0:T(8,128)} %bitcast.11, s32[384]{0:T(512)} %rmask_hbm.1, bf16[576,128]{1,0:T(8,128)(2,1)} %bitcast.8, bf16[32,256]{1,0:T(8,128)(2,1)} %bitcast.9, bf16[32,256]{1,0:T(8,128)(2,1)} %bitcast.10, bf16[1024,128]{1,0:T(8,128)(2,1)} %oproj_hbm.1, ...), custom_call_target="tpu_custom_call" | custom-call | flops 1500000000 | bytes 2000000 | tf_op jit(solution)/shard_map/pallas_call | solution.py:632
  73.6 1.6 %copy.14 = bf16[24,24,128]{2,1,0:T(8,128)(2,1)} copy(bf16[24,24,128]{2,1,0:T(8,128)(2,1)} %bitcast.6) | data formatting | bytes 294912

commit v5 on v4

--- a/solution.py
+++ b/solution.py
@@ -74,7 +74,6 @@
     yp, ym = (r, col_of(zl, y + 1, core)), (r, col_of(zl, y - 1, core))
     zlo = (r, col_of(1 - zl, y, core))
     twin = (r, col_of(zl, y, 1 - core))
-    dp, dm = (r, col_of(1 - zl, y + 1, core)), (r, col_of(1 - zl, y - 1, core))
 
     barrier = pltpu.get_barrier_semaphore()
     def greet(t, carry):
@@ -98,7 +97,7 @@
 
     for t in range(4):
         greet_tri(t, 0)
-    for device in (zp, zm, xp, xm, yp, ym, zlo, twin, dp, dm):
+    for device in (zp, zm, xp, xm, yp, ym, zlo, twin):
         pl.semaphore_signal(barrier, inc=1, device_id=device, device_id_type=MESH)
 
     for load in loads.values():
@@ -222,8 +221,8 @@
             wait_send(self.half(self.pos(1), 1), self.k + 3)
 
     class Columns:
-        def __init__(self, ref, half_rows, k, diagonal):
-            self.ref, self.k, self.diagonal = ref, k, diagonal
+        def __init__(self, ref, half_rows, k):
+            self.ref, self.k = ref, k
 
             def slot(ll):
                 return lambda yy: ref.at[col_of(ll, yy, core)]
@@ -248,15 +247,11 @@
         def start(self):
             send(self.ref.at[q], self.k, zlo)
             self.rings[0].start()
-            if self.diagonal:
-                send(self.ref.at[q], self.rings[1].k, dp)
-                send(self.ref.at[q], self.rings[1].k + 1, dm)
             self.to_twin(zl, y)
 
         def other_half(self):
             wait_recv(self.ref.at[col_of(1 - zl, y, core)], self.k)
-            if not self.diagonal:
-                self.rings[1].start()
+            self.rings[1].start()
             self.to_twin(1 - zl, y)
 
         def from_minus(self, e):
@@ -334,10 +329,10 @@
         lambda zz, xx, h: right_all.at[right_rows(zz, xx, h, 16)],
         RIGHT_GATHER,
     )
-    left_columns = Columns(left_all, 2, LEFT_GATHER, True)
+    left_columns = Columns(left_all, 2, LEFT_GATHER)
 
     def zero_chunk(t, carry):
-        bd[pl.ds(pl.multiple_of(t * 128, 128), 128), :] = jnp.zeros((128, 512), BF16)
+        bd[pl.ds(pl.multiple_of(t * 64, 64), 64), :] = jnp.zeros((64, 256), BF16)
         part[pl.ds(pl.multiple_of(t * 144, 144), 144), :] = jnp.zeros((144, 128), F32)
         return carry
 
@@ -346,8 +341,8 @@
 
     def fill_chunk(t, carry):
         block = oproj_ref[pl.ds(pl.multiple_of(t * 32, 32), 32), :]
-        for u in range(4):
-            bd[pl.ds(pl.multiple_of(t * 128 + 32 * u, 32), 32), 128 * u : 128 * u + 128] = block
+        for u in range(2):
+            bd[pl.ds(pl.multiple_of(t * 64 + 32 * u, 32), 32), 128 * u : 128 * u + 128] = block
         return carry
 
     lax.fori_loop(0, 32, fill_chunk, 0)
@@ -361,7 +356,7 @@
     for name in ("pair", "tproj", "tgate", "tout", "tin", "trans"):
         loads[name].wait()
 
-    pl.semaphore_wait(barrier, 18 - 2 * same.astype(I32))
+    pl.semaphore_wait(barrier, 16 - 2 * same.astype(I32))
 
     def scatter(t, carry):
         is_self = same & (t == z)
@@ -405,13 +400,19 @@
     left_columns.finish(0)
     right_rows_gather.x_neighbours(3)
     left_columns.finish(1)
-    left_columns.finish_twin()
-
-    for g in range(6):
-        for m in range(4):
-            left_t[128 * g : 128 * g + 128, 128 * m : 128 * m + 128] = (
+
+    def turn(m):
+        lanes = pl.ds(pl.multiple_of(m * 128, 128), 128)
+        for g in range(6):
+            left_t[128 * g : 128 * g + 128, lanes] = (
                 left_all[4 * (g // 2) + m, :, g % 2].reshape(128, 128).T
             )
+
+    turn(core)
+    turn(core + 2)
+    left_columns.finish_twin()
+    turn(1 - core)
+    turn(3 - core)
     for e in range(4):
         right_rows_gather.x_far(e)
 
@@ -423,15 +424,23 @@
         for m in range(4)
     )
     counts = jnp.maximum(counts[:24], 1.0)
+    low = lax.broadcasted_iota(I32, (24, 128), 1) < 64
     for g in range(3):
         outer = dot(left_t[...], right_all[:, 256 * g : 256 * g + 256])
         for u in range(2):
-            for c in range(32):
-                lhs2[32 * (2 * g + u) : 32 * (2 * g + u) + 24, 128 * c : 128 * c + 128] = outer[
-                    24 * c : 24 * c + 24, 128 * u : 128 * u + 128
-                ].astype(BF16)
+            tile = outer[:, 128 * u : 128 * u + 128]
+            turned = pltpu.roll(tile, 64, 1)
+            at = 32 * (2 * g + u)
+            for c in range(0, 32, 2):
+                even, odd = slice(24 * c, 24 * c + 24), slice(24 * c + 24, 24 * c + 48)
+                lanes = slice(64 * c, 64 * c + 128)
+                lhs2[at : at + 24, lanes] = jnp.where(low, tile[even], turned[odd]).astype(BF16)
+                lhs2[192 + at : 192 + at + 24, lanes] = jnp.where(
+                    low, turned[even], tile[odd]
+                ).astype(BF16)
+    both_proj = dot(lhs2[...], bd[...])
     for n in range(2):
-        proj = dot(lhs2[...], bd[:, 256 * n : 256 * n + 256])
+        proj = both_proj[192 * n : 192 * n + 192]
         for g in range(6):
             for u in range(2):
                 j = 4 * g + 2 * n + u
@@ -446,12 +455,7 @@
         first[rows, :] = rounded
         normed[rows, :] = norm(rounded).astype(BF16)
 
-    for t in range(3):
-        rows = slice(192 * t, 192 * t + 192)
-        p = dot(normed[rows, :], tproj_ref[:, 256:])
-        tri_send[rows, :] = (jax.nn.sigmoid(p[:, :128]) * p[:, 128:] * pmask[rows, :]).astype(BF16)
-
-    tri_columns = Columns(tri_left, 288, TRI_LEFT, False)
+    tri_columns = Columns(tri_left, 288, TRI_LEFT)
 
     def chunk(n):
         return Rows(
@@ -465,7 +469,7 @@
 
     def tri_scatter(t, carry):
         is_self = same & (t == z)
-        piece = pl.ds(pl.multiple_of(t * 144, 144), 144)
+        piece = pl.ds(t * 144, 144)
 
         @pl.when(jnp.logical_not(is_self))
         def _():
@@ -480,7 +484,12 @@
 
         return carry
 
-    lax.fori_loop(0, 4, tri_scatter, 0)
+    for t in range(3):
+        rows = slice(192 * t, 192 * t + 192)
+        p = dot(normed[rows, :], tproj_ref[:, 256:])
+        tri_send[rows, :] = (jax.nn.sigmoid(p[:, :128]) * p[:, 128:] * pmask[rows, :]).astype(BF16)
+    for t in range(4):
+        tri_scatter(t, 0)
     for t in range(3):
         rows = slice(192 * t, 192 * t + 192)
         p = dot(normed[rows, :], tproj_ref[:, :256])
@@ -512,19 +521,19 @@
 
         lax.fori_loop(0, 16, widen, 0)
 
-    def accumulate(xx, zz):
+    def accumulate(xx, zz, first_block=0, last_block=4):
         def widen(t, carry):
             rf[t] = tri_right[xx, zz, t].astype(F32)
             return carry
 
-        lax.fori_loop(0, 4, widen, 0)
+        lax.fori_loop(first_block, last_block, widen, 0)
 
         def block(t, carry):
             def at(u, v):
                 return pl.ds(pl.multiple_of(((t * 4 + u) * 24 + zz * 6 + v) * 8, 8), 8)
 
             acc = [[part[at(u, v), :] for v in range(6)] for u in range(4)]
-            for b in range(4):
+            for b in range(first_block, last_block):
                 for k in range(3):
                     left = [
                         lf[xx, b, pl.ds(pl.multiple_of((t * 4 + u) * 24 + 8 * k, 8), 8), :]
@@ -585,8 +594,9 @@
     accumulate(xat(-1), order[3])
     accumulate(xat(1), order[3])
     rows0.x_far(3)
+    accumulate(xat(2), order[3], 0, 2)
     rows1.x_far(3)
-    accumulate(xat(2), order[3])
+    accumulate(xat(2), order[3], 2, 4)
 
     for t in range(1):
         rows = slice(576 * t, 576 * t + 576)
@@ -650,13 +660,13 @@
             pltpu.VMEM((2, 768, 128), F32),
             pltpu.VMEM((1024, 256), BF16),
             pltpu.VMEM((768, 768), BF16),
-            pltpu.VMEM((4096, 512), BF16),
+            pltpu.VMEM((2048, 256), BF16),
             pltpu.VMEM((32, 768), BF16),
             pltpu.VMEM((4, 2, 32, 128), BF16),
             pltpu.VMEM((16, 4, 2, 32, 128), BF16),
             pltpu.VMEM((512, 896), BF16),
             pltpu.VMEM((768, 512), BF16),
-            pltpu.VMEM((192, 4096), BF16),
+            pltpu.VMEM((384, 2048), BF16),
             pltpu.VMEM((576, 128), F32),
             pltpu.VMEM((576, 128), F32),
             pltpu.VMEM((576, 128), BF16),

time: 76.2 us -> 73.8 us (0.969)
  Pallas kernels: 73.6 us -> 71.5 us
    pallas_call x1, Pallas kernels: 73.6 us -> 71.5 us  [shards(): pl.pallas_call(kernel, out_shape=jax.ShapeDtypeStruct((576, 128), BF16),...]
where the time goes in v5:
time: 73.8 us; the launch traced here: 73.1 us
  Pallas kernels  71.5 us (97%)
  local copies, waits for them, and re-layouts  1.59 us (2%)
    pallas_call x1, Pallas kernels, shards(): pl.pallas_call(kernel, out_shape=jax.ShapeDtypeStruct((576, 128), BF16),...  71.5 us
    unnamed x1, local copies, waits for them, and re-layouts  1.59 us

profile of v5, /device:TPU:1, one launch (start us, length us, event | category | flops | bytes accessed | tf_op | source)
XLA Modules:
  0.0 73.1 jit_solution(7523757661155728959)
XLA Ops:
  0.0 71.5 %shard_map.118 = bf16[576,128]{1,0:T(8,128)(2,1)} custom-call(bf16[768,256]{1,0:T(8,128)(2,1)} %bitcast.7, s32[24,32]{1,0:T(8,128)} %bitcast.11, s32[384]{0:T(512)} %rmask_hbm.1, bf16[576,128]{1,0:T(8,128)(2,1)} %bitcast.8, bf16[32,256]{1,0:T(8,128)(2,1)} %bitcast.9, bf16[32,256]{1,0:T(8,128)(2,1)} %bitcast.10, bf16[1024,128]{1,0:T(8,128)(2,1)} %oproj_hbm.1, ...), custom_call_target="tpu_custom_call" | custom-call | flops 1500000000 | bytes 2000000 | tf_op jit(solution)/shard_map/pallas_call | solution.py:642
  71.5 1.6 %copy.14 = bf16[24,24,128]{2,1,0:T(8,128)(2,1)} copy(bf16[24,24,128]{2,1,0:T(8,128)(2,1)} %bitcast.6) | data formatting | bytes 294912

commit v6 on v5

--- a/solution.py
+++ b/solution.py
@@ -387,8 +387,8 @@
 
     lax.fori_loop(0, 4, scatter_arrived, 0)
     left_columns.start()
+    left_columns.other_half()
     right_rows_gather.z_neighbours()
-    left_columns.other_half()
     left_columns.from_minus(0)
     left_columns.from_plus(0)
     right_rows_gather.x_neighbours(0)

time: 73.8 us -> 75.1 us (1.018)
  Pallas kernels: 71.5 us -> 72.4 us
    pallas_call x1, Pallas kernels: 71.5 us -> 72.4 us  [shards(): pl.pallas_call(kernel, out_shape=jax.ShapeDtypeStruct((576, 128), BF16),...]
where the time goes in v6:
time: 75.1 us; the launch traced here: 74 us
  Pallas kernels  72.4 us (96%)
  local copies, waits for them, and re-layouts  1.59 us (2%)
    pallas_call x1, Pallas kernels, shards(): pl.pallas_call(kernel, out_shape=jax.ShapeDtypeStruct((576, 128), BF16),...  72.4 us
    unnamed x1, local copies, waits for them, and re-layouts  1.59 us

profile of v6, /device:TPU:1, one launch (start us, length us, event | category | flops | bytes accessed | tf_op | source)
XLA Modules:
  0.0 74.0 jit_solution(1071242910045520483)
XLA Ops:
  0.0 72.4 %shard_map.118 = bf16[576,128]{1,0:T(8,128)(2,1)} custom-call(bf16[768,256]{1,0:T(8,128)(2,1)} %bitcast.7, s32[24,32]{1,0:T(8,128)} %bitcast.11, s32[384]{0:T(512)} %rmask_hbm.1, bf16[576,128]{1,0:T(8,128)(2,1)} %bitcast.8, bf16[32,256]{1,0:T(8,128)(2,1)} %bitcast.9, bf16[32,256]{1,0:T(8,128)(2,1)} %bitcast.10, bf16[1024,128]{1,0:T(8,128)(2,1)} %oproj_hbm.1, ...), custom_call_target="tpu_custom_call" | custom-call | flops 1500000000 | bytes 2000000 | tf_op jit(solution)/shard_map/pallas_call | solution.py:642
  72.4 1.6 %copy.14 = bf16[24,24,128]{2,1,0:T(8,128)(2,1)} copy(bf16[24,24,128]{2,1,0:T(8,128)(2,1)} %bitcast.6) | data formatting | bytes 294912
